TPU v7x, 256 devices: a whole 4x4x8 slice. The times are simulated.
256 devices in a mesh: dp: 64 (over z, x, core), space: 2 (over y_hi), chan: 2 (over y_lo).
Axes of the slice: x: 4, y: 4 (y_hi: 2, y_lo: 2; y = y_hi * 2 + y_lo), z: 8, core: 2. Of those that a mesh axis runs over, the one named last changes fastest.
Arguments:
- images: bfloat16 [64, 32, 256, 512], P('dp', ('space', 'chan')), may hold values from -6 to 6
- reduce_weight: bfloat16 [512, 256], replicated, may hold values from -0.375 to 0.375
- spatial_weight: bfloat16 [3, 3, 256, 256], replicated, may hold values from -0.1875 to 0.1875
- expand_weight: bfloat16 [768, 1024], P(None, ('space', 'chan')), may hold values from -0.21875 to 0.21875
- cotangent: bfloat16 [64, 16, 128, 1024], P('dp', None, None, ('space', 'chan')), may hold values from -6 to 6
Outputs:
- output: bfloat16 [64, 16, 128, 1024], P('dp', None, None, ('space', 'chan'))
- input_grad: bfloat16 [64, 32, 256, 512], P('dp', ('space', 'chan'))
- reduce_grad: float32 [512, 256], replicated
- spatial_grad: float32 [3, 3, 256, 256], replicated
- expand_grad: float32 [768, 1024], P(None, ('space', 'chan'))
All inputs are finite; a program needn't handle non-finite values.
Results may differ from a plain program's by a relative error of at most 0.0067.
Values may be sent and summed in bfloat16 or wider, within the bound.
A program may use at most 128 MiB of HBM per device.

v0:
```python
import math

import jax
import jax.numpy as jnp
from jax import lax
from jax.sharding import PartitionSpec as P


def from_behind(array, axis, by):
    count = lax.axis_size(axis)
    pairs = [(i, i + by) for i in range(count) if 0 <= i + by < count]
    return lax.ppermute(array, axis, pairs)


def silu_value(pre):
    return pre * jax.nn.sigmoid(pre)


def silu_slope(pre):
    sigma = jax.nn.sigmoid(pre)
    return sigma * (1.0 + pre * (1.0 - sigma))


def taps(padded, rows, cols):
    return [
        padded[row_off : row_off + rows : 2, col_off : col_off + cols : 2]
        for row_off in range(3)
        for col_off in range(3)
    ]


def pad_axis(array, axis, before, after):
    widths = [(0, 0)] * array.ndim
    widths[axis] = (before, after)
    return jnp.pad(array, widths)


def weave_odd(even_part, odd_part, axis):
    odd_full = pad_axis(odd_part, axis, 0, 1)
    woven = jnp.stack([even_part, odd_full], axis=axis + 1)
    shape = list(even_part.shape)
    count = shape[axis]
    shape[axis] = 2 * count
    woven = woven.reshape(shape)
    return lax.slice_in_dim(woven, 0, 2 * count - 1, axis=axis)


def fold_taps(first, second, third, axis):
    even_part = pad_axis(first, axis, 0, 1) + pad_axis(third, axis, 1, 0)
    return weave_odd(even_part, second, axis)


def spread_back(grad_out, spatial_weight):
    columns_done = []
    for col_off in range(3):
        parts = [
            jnp.dot(
                grad_out, spatial_weight[row_off, col_off].T, preferred_element_type=jnp.float32
            )
            for row_off in range(3)
        ]
        columns_done.append(fold_taps(parts[0], parts[1], parts[2], 0))
    return fold_taps(columns_done[0], columns_done[1], columns_done[2], 1)


def place_even(small):
    half_rows, half_cols, chans = small.shape
    empty = jnp.zeros_like(small)
    wide = jnp.stack([small, empty], axis=2).reshape(half_rows, 2 * half_cols, chans)
    return jnp.stack([wide, jnp.zeros_like(wide)], axis=1).reshape(
        2 * half_rows, 2 * half_cols, chans
    )


def body(images, reduce_weight, spatial_weight, expand_weight, cotangent):
    image = images[0]
    cot_block = cotangent[0]
    rows = image.shape[0]
    cols = image.shape[1]
    middle = reduce_weight.shape[1]
    reduce_pre = jnp.dot(image, reduce_weight, preferred_element_type=jnp.float32)
    reduced = silu_value(reduce_pre).astype(jnp.bfloat16)
    above = from_behind(reduced[-1:], ("space", "chan"), 1)
    padded = jnp.pad(jnp.concatenate([above, reduced], axis=0), ((0, 0), (1, 0), (0, 0)))
    windows = taps(padded, rows, cols)
    spatial_pre = jnp.zeros((rows // 2, cols // 2, middle), jnp.float32)
    for tap_index in range(9):
        spatial_pre = spatial_pre + jnp.dot(
            windows[tap_index],
            spatial_weight[tap_index // 3, tap_index % 3],
            preferred_element_type=jnp.float32,
        )
    spatial = silu_value(spatial_pre).astype(jnp.bfloat16)
    stacked = jnp.concatenate([spatial, image[::2, ::2]], axis=-1)
    stacked_all = lax.all_gather(stacked, ("space", "chan"), axis=0, tiled=True)
    expand_pre = jnp.dot(stacked_all, expand_weight, preferred_element_type=jnp.float32)
    output = silu_value(expand_pre).astype(jnp.bfloat16)
    grad_pre = (cot_block.astype(jnp.float32) * silu_slope(expand_pre)).astype(jnp.bfloat16)
    expand_part = jnp.dot(
        stacked_all.reshape(-1, stacked_all.shape[-1]).T,
        grad_pre.reshape(-1, grad_pre.shape[-1]),
        preferred_element_type=jnp.float32,
    )
    stacked_grad = lax.psum_scatter(
        jnp.dot(grad_pre, expand_weight.T, preferred_element_type=jnp.float32),
        ("space", "chan"),
        scatter_dimension=0,
        tiled=True,
    )
    expand_total = lax.psum(expand_part, "dp")
    spatial_grad_pre = (stacked_grad[..., :middle] * silu_slope(spatial_pre)).astype(jnp.bfloat16)
    flat_spatial = spatial_grad_pre.reshape(-1, middle)
    spatial_term = jnp.stack(
        [
            jnp.dot(window.reshape(-1, middle).T, flat_spatial, preferred_element_type=jnp.float32)
            for window in windows
        ]
    ).reshape(3, 3, middle, middle)
    canvas = spread_back(spatial_grad_pre, spatial_weight)
    below = from_behind(canvas[0:1, 1:], ("space", "chan"), -1)
    reduced_grad = jnp.concatenate([canvas[1:-1, 1:], canvas[-1:, 1:] + below], axis=0)
    reduce_grad_pre = (reduced_grad * silu_slope(reduce_pre)).astype(jnp.bfloat16)
    reduce_term = jnp.dot(
        image.reshape(-1, image.shape[-1]).T,
        reduce_grad_pre.reshape(-1, middle),
        preferred_element_type=jnp.float32,
    )
    input_full = jnp.dot(reduce_grad_pre, reduce_weight.T, preferred_element_type=jnp.float32)
    input_full = input_full + place_even(stacked_grad[..., middle:])
    reduce_total, spatial_total = lax.psum((reduce_term, spatial_term), ("dp", "space", "chan"))
    scale = 1.0 / math.sqrt(lax.axis_size("dp") * cot_block.shape[0] * cot_block.shape[1])
    return (
        output[None],
        input_full.astype(jnp.bfloat16)[None],
        reduce_total * scale,
        spatial_total * scale,
        expand_total * scale,
    )


def solution(mesh):
    return jax.shard_map(
        body,
        mesh=mesh,
        in_specs=(
            P("dp", ("space", "chan"), None, None),
            P(),
            P(),
            P(None, ("space", "chan")),
            P("dp", None, None, ("space", "chan")),
        ),
        out_specs=(
            P("dp", None, None, ("space", "chan")),
            P("dp", ("space", "chan"), None, None),
            P(),
            P(),
            P(None, ("space", "chan")),
        ),
        check_vma=False,
    )
```

profile of v0, /device:TPU:1, one launch (start us, length us, event | category | flops | bytes accessed | tf_op | source)
XLA Modules:
  0.0 636.8 jit_solution(9317387328081174092)
XLA Ops:
  7.2 3.7 multiply_convert_fusion.1
  10.9 4.0 collective-permute-start
  14.9 7.4 %slice.116 = bf16[4,128,512]{2,1,0:T(8,128)(2,1)} slice(bf16[8,256,512]{2,1,0:T(8,128)(2,1)} %bitcast.218), slice={[0:8:2], [0:256:2], [0:512:1]} | slice | bytes 1048576 | tf_op jit(solution)/shard_map/slice | solution.py:94
  23.2 2.7 slice.110
  25.9 2.7 slice.108
  28.6 2.7 slice.106
  31.3 2.7 slice.104
  34.0 2.7 slice.102
  37.1 2.7 slice.98
  39.8 2.8 slice.114
  42.8 1.2 convolution_add_fusion.10
  46.0 1.0 multiply_convert_fusion.2
  48.0 45.2 %all-gather.2.cloned.1.call-done = bf16[16,128,768]{2,1,0:T(8,128)(2,1)} async-done(((bf16[4,128,768]{2,1,0:T(8,128)(2,1)}), bf16[16,128,768]{2,1,0:T(8,128)(2,1)}) %all-gather.2.cloned.1.call-update) | async-done | bytes 3145744 | tf_op jit(solution)/shard_map/all_gather | solution.py:95
  93.2 2.9 fusion.23
  96.1 6.1 fusion.21
  102.3 4.3 convolution_bitcast_fusion
  106.8 62.3 %reduce-scatter.2.cloned.1.call-done = f32[4,128,768]{2,1,0:T(8,128)} async-done(((f32[16,128,768]{2,1,0:T(8,128)}), f32[4,128,768]{2,1,0:T(8,128)}) %reduce-scatter.2.cloned.1.call-update) | async-done | bytes 1572880 | tf_op jit(solution)/shard_map/reduce_scatter | solution.py:104
  169.2 1.4 fusion.20
  175.6 1.2 copy.41
  176.8 3.1 reshape.48
  179.9 1.0 slice.132
  180.9 1.6 collective-permute-start.1
  183.6 1.9 fusion.16
  193.7 1.5 convolution_bitcast_fusion.1
  195.2 1.6 copy-done.4
  196.8 1.5 fusion.19
  198.3 156.6 %all-reduce.19.cloned.1.call-done = f32[768,256]{1,0:T(8,128)} async-done(((f32[768,256]{1,0:T(8,128)}), f32[768,256]{1,0:T(8,128)}) %all-reduce.19.cloned.1.call-update) | async-done | bytes 786448 | tf_op jit(solution)/shard_map/psum | solution.py:110
  354.9 2.1 broadcast_multiply_fusion.1
  360.1 2.2 fusion.5
  362.2 262.6 %all-reduce.21.cloned.1.call-done = (f32[512,256]{0,1:T(8,128)}, f32[3,3,256,256]{3,2,1,0:T(8,128)}) async-done(((f32[512,256]{0,1:T(8,128)}, f32[3,3,256,256]{3,2,1,0:T(8,128)}), (f32[512,256]{0,1:T(8,128)}, f32[3,3,256,256]{3,2,1,0:T(8,128)})) %all-reduce.21.cloned.1.call-update) | async-done | bytes 2883600 | tf_op jit(solution)/shard_map/psum | solution.py:130
  624.8 1.1 broadcast_multiply_fusion.2
  626.9 3.3 broadcast_multiply_fusion
  (109 shorter events, 22.7 us)
Async XLA Ops:
  7.2 86.1 %copy-start = (bf16[768,256]{1,0:T(8,128)(2,1)S(1)}, bf16[768,256]{1,0:T(8,128)(2,1)}, u32[]{:S(2)}) copy-start(bf16[768,256]{1,0:T(8,128)(2,1)} %param.8) | copy-start | bytes 1179652
  7.2 86.0 %all-gather.2.cloned.1.call-start = ((), (), s32[]{:S(2)}) async-start(), calls=%async_computation.1 | async-start | bytes 3932160 | tf_op jit(solution)/shard_map/all_gather | solution.py:95
  10.9 11.5 %collective-permute-start = (bf16[1,256,256]{2,1,0:T(8,128)(2,1)S(1)}, bf16[1,256,256]{2,1,0:T(8,128)(2,1)S(1)}, u32[]{:S(2)}, u32[]{:S(2)}) collective-permute-start(bf16[1,256,256]{2,1,0:T(8,128)(2,1)S(1)} %slice.125), channel_id=1, source_target_pairs={{0,1},{1,2},{2,3},{4,5},{5,6},{6,7},{8,9},{9,10},{10,11},{12,13},{... | collective-permute-start | bytes 393224 | tf_op jit(solution)/shard_map/ppermute | solution.py:12
  23.1 19.4 %copy-start.5 = (bf16[3,3,256,256]{3,2,1,0:T(8,128)(2,1)S(1)}, bf16[3,3,256,256]{3,2,1,0:T(8,128)(2,1)}, u32[]{:S(2)}) copy-start(bf16[3,3,256,256]{3,2,1,0:T(8,128)(2,1)} %param.7) | copy-start | bytes 3538948
  42.6 1.5 copy-start.15
  42.6 1.7 copy-start.13
  42.8 1.7 copy-start.11
  44.1 1.0 copy-start.9
  44.3 1.0 copy-start.7
  45.0 1.0 copy-start.20
  45.5 1.5 copy-start.17
  48.0 121.2 %reduce-scatter.2.cloned.1.call-start = ((), (), s32[]{:S(2)}) async-start(), calls=%async_computation.2 | async-start | bytes 7864320 | tf_op jit(solution)/shard_map/reduce_scatter | solution.py:104
  96.1 6.2 copy-start.3
  102.2 252.7 %all-reduce.19.cloned.1.call-start = ((), (), s32[]{:S(2)}) async-start(), calls=%async_computation.3 | async-start | bytes 1572864 | tf_op jit(solution)/shard_map/psum | solution.py:110
  106.6 64.0 %copy-start.6 = (bf16[3,3,256,256]{3,2,1,0:T(8,128)(2,1)S(1)}, bf16[3,3,256,256]{3,2,1,0:T(8,128)(2,1)}, u32[]{:S(2)}) copy-start(bf16[3,3,256,256]{3,2,1,0:T(8,128)(2,1)} %param.7) | copy-start | bytes 3538948
  106.6 518.2 %all-reduce.21.cloned.1.call-start = ((), (), s32[]{:S(2)}) async-start(), calls=%async_computation.4 | async-start | bytes 5767168 | tf_op jit(solution)/shard_map/psum | solution.py:130
  170.8 1.3 copy-start.16
  179.9 5.6 copy-start.14
  179.9 6.6 %copy-start.12 = (bf16[4,128,256]{2,1,0:T(8,128)(2,1)S(1)}, bf16[4,128,256]{2,1,0:T(8,128)(2,1)}, u32[]{:S(2)}) copy-start(bf16[4,128,256]{2,1,0:T(8,128)(2,1)} %slice.106) | copy-start | bytes 786436
  179.9 7.6 %copy-start.10 = (bf16[4,128,256]{2,1,0:T(8,128)(2,1)S(1)}, bf16[4,128,256]{2,1,0:T(8,128)(2,1)}, u32[]{:S(2)}) copy-start(bf16[4,128,256]{2,1,0:T(8,128)(2,1)} %slice.108) | copy-start | bytes 786436
  180.9 7.5 %copy-start.8 = (bf16[4,128,256]{2,1,0:T(8,128)(2,1)S(1)}, bf16[4,128,256]{2,1,0:T(8,128)(2,1)}, u32[]{:S(2)}) copy-start(bf16[4,128,256]{2,1,0:T(8,128)(2,1)} %slice.110) | copy-start | bytes 786436
  180.9 10.6 %collective-permute-start.1 = (f32[1,256,256]{2,1,0:T(8,128)S(1)}, f32[1,256,256]{2,1,0:T(8,128)S(1)}, u32[]{:S(2)}, u32[]{:S(2)}) collective-permute-start(f32[1,256,256]{2,1,0:T(8,128)S(1)} %slice.132), channel_id=1, source_target_pairs={{1,0},{2,1},{3,2},{5,4},{6,5},{7,6},{9,8},{10,9},{11,10},{13,12},{... | collective-permute-start | bytes 786440 | tf_op jit(solution)/shard_map/ppermute | solution.py:12
  185.5 4.9 copy-start.2
  189.4 1.1 copy-start.21
  190.4 1.7 copy-start.18
  192.1 1.6 copy-start.23
  195.2 1.6 copy-start.4
  198.3 158.7 %copy-start.19 = (f32[4,128,768]{2,1,0:T(8,128)S(1)}, f32[4,128,768]{2,1,0:T(8,128)}, u32[]{:S(2)}) copy-start(f32[4,128,768]{2,1,0:T(8,128)} %reduce-scatter.2.cloned.1.call-done) | copy-start | bytes 4718596
  359.1 1.0 copy-start.22
  626.9 3.3 copy-start.1
Sparse Core Ops, SparseCore 0:
  48.1 45.0 all-gather.1
  102.4 66.7 reduce-scatter.1
  173.2 181.7 all-reduce.18
  362.0 262.7 all-reduce.20
where the time goes:
time: 638 us; the launch traced here: 637 us
  waiting for transfers between devices  527 us (83%)
  local copies, waits for them, and re-layouts  41 us (6%)
  matrix products  36.5 us (6%)
  between operations  14.3 us (2%)
  other arithmetic  12.2 us (2%)
    psum x1, waiting for transfers between devices, body(): lax.psum((reduce_term, spatial_term), ('dp', 'space', 'chan'))  263 us
    psum x1, waiting for transfers between devices, body(): expand_total = lax.psum(expand_part, 'dp')  157 us
    reduce_scatter x1, waiting for transfers between devices, body(): lax.psum_scatter(jnp.dot(grad_pre, expand_weight.T, preferred_element_typ...  62.3 us
    all_gather x1, waiting for transfers between devices, body(): stacked_all = lax.all_gather(stacked, ('space', 'chan'), axis=0, tiled=True)  45.2 us
    slice x9, local copies, waits for them, and re-layouts, taps(): padded[row_off:row_off + rows:2, col_off:col_off + cols:2]  19.9 us
  transfers between devices with their start and end apart: 6, of which 4 were waited for; matrix products, arithmetic and copies ran while one was open for 7% of the time, Pallas kernels for 0%

commit v1 on v0

v1 whole, which is shorter than its diff:
```python
import functools
import math

import jax
import jax.numpy as jnp
from jax import lax
from jax.experimental import pallas as pl
from jax.experimental.pallas import tpu as pltpu
from jax.sharding import PartitionSpec as P

MESH = pl.DeviceIdType.MESH
F32 = jnp.float32
BF16 = jnp.bfloat16


def sigmoid(pre):
    return 1.0 / (1.0 + jnp.exp(-pre))


def slope_of(pre, sig):
    return sig * (1.0 + pre * (1.0 - sig))


def dot(left, right):
    return jnp.dot(left, right, preferred_element_type=F32)


def dot_tn(left, right):
    return lax.dot_general(left, right, (((0,), (0,)), ((), ())), preferred_element_type=F32)


def dot_nt(left, right):
    return lax.dot_general(left, right, (((1,), (1,)), ((), ())), preferred_element_type=F32)


def loop(low, high, step_fn):
    def step(index, carry):
        step_fn(index)
        return carry

    lax.fori_loop(low, high, step, 0)


def block_kernel(
    nx, nz, img, wr, ws, we, cot,
    out, igrad, rgrad, sgrad, egrad,
    wg, cotr, a_s, pre_s, rowbuf, spre_s, stk, obuf, stg, sgp, sgq, sbuf, rg_s, rgp_s, rterm, widebuf,
    e_send, e_rc, e_p, e_rp, e_z, e_rz, e_f, e_g, e_out,
    s_send, s_rc, s_p, s_rp, r_send, r_rc, r_p, r_rp, t_z, t_rz, t_f, t_g, t_out,
    y_send_sem, y_recv_sem, p_send_sem, p_recv_sem, z_send_sem, z_recv_sem, c_send_sem, c_recv_sem,
):
    rows, cols, chans = img.shape
    half_cols = cols // 2
    half_rows = rows // 2
    mid = wr.shape[1]
    stack_ch, filt = we.shape
    pix = half_rows * half_cols
    lanes = 128
    planes = nx * 4
    dp = lax.axis_index("dp")
    y = lax.axis_index("space") * 2 + lax.axis_index("chan")
    core = dp % 2
    x = (dp // 2) % nx
    z = dp // (2 * nx)
    plane = x * 4 + y
    scale = 1.0 / math.sqrt(lax.axis_size("dp") * cot.shape[0] * pix)

    def device(z_at, x_at, core_at, y_at):
        return ((z_at * nx + x_at) * 2 + core_at, y_at // 2, y_at % 2)

    def at_y(y_at):
        return device(z, x, core, y_at)

    def at_x(x_at):
        return device(z, x_at, core, y)

    def at_z(z_at):
        return device(z_at, x, core, y)

    def at_plane(place):
        return device(z, place // 4, core, place % 4)

    other_core = device(z, x, 1 - core, y)

    def remote(src, dst, send_sem, recv_sem, target):
        return pltpu.make_async_remote_copy(
            src_ref=src, dst_ref=dst, send_sem=send_sem, recv_sem=recv_sem, device_id=target, device_id_type=MESH
        )

    barrier = pltpu.get_barrier_semaphore()
    pl.semaphore_signal(barrier, inc=1, device_id=other_core, device_id_type=MESH)

    def greet_plane(k):
        pl.semaphore_signal(barrier, inc=1, device_id=at_plane((plane + k) % planes), device_id_type=MESH)

    def greet_z(k):
        pl.semaphore_signal(barrier, inc=1, device_id=at_z((z + k) % nz), device_id_type=MESH)

    loop(1, planes, greet_plane)
    loop(1, nz, greet_z)

    rowbuf[:, 0:8] = jnp.zeros((mid // lanes, 8, lanes), F32)

    def reduce_row(p):
        pre = dot(img[p], wr[...])
        pre_s[p] = pre
        reduced = pre * sigmoid(pre)
        a_par, a_idx = (p + 1) % 2, (p + 1) // 2
        for block in range(mid // lanes):
            rowbuf[block, 8 : 8 + cols] = reduced[:, block * lanes : (block + 1) * lanes]
            for part, start in enumerate((7, 8, 9)):
                lane = part * mid + block * lanes
                a_s[a_par, a_idx, :, lane : lane + lanes] = rowbuf[block, pl.ds(start, half_cols, stride=2), :].astype(BF16)

    reduce_row(rows - 1)
    pl.semaphore_wait(barrier, planes + nz - 1)

    halo_row = remote(
        a_s.at[0, half_rows], a_s.at[0, 0], y_send_sem.at[12], y_recv_sem.at[12], at_y((y + 1) % 4)
    )

    @pl.when(y < 3)
    def _():
        halo_row.start()

    part_rows = stack_ch // (2 * nx)
    part = pl.ds(pl.multiple_of((core * nx + x) * part_rows, part_rows), part_rows)
    half_part = pl.ds(pl.multiple_of(core * (stack_ch // 2), stack_ch // 2), stack_ch // 2)

    def weight_y(k):
        return remote(we.at[part], wg.at[k, part], y_send_sem.at[k], y_recv_sem.at[k], at_y((y + k) % 4))

    def weight_x(k):
        return remote(
            wg.at[1:4, part], wg.at[1:4, part], z_send_sem.at[3 * nz + k], z_recv_sem.at[3 * nz + k], at_x((x + k) % nx)
        )

    weight_core = remote(wg.at[1:4, half_part], wg.at[1:4, half_part], c_send_sem.at[0], c_recv_sem.at[0], other_core)

    def cot_y(k):
        return remote(
            cot.at[(y + k) % 4], cotr.at[k], y_send_sem.at[4 + k], y_recv_sem.at[4 + k], at_y((y + k) % 4)
        )

    loop(1, 4, lambda k: weight_y(k).start())
    loop(1, 4, lambda k: cot_y(k).start())

    wg[0] = we[...]
    cotr[0] = cot[y]
    loop(0, 2, reduce_row)
    loop(1, 4, lambda k: weight_y(k).wait_recv())
    loop(1, nx, lambda k: weight_x(k).start())
    loop(2, rows - 1, reduce_row)

    take = (
        lax.broadcasted_iota(jnp.int32, (half_cols, cols), 1)
        == 2 * lax.broadcasted_iota(jnp.int32, (half_cols, cols), 0)
    ).astype(F32).astype(BF16)

    def pick_even(i):
        stk[i, :, mid : mid + chans] = dot(take, img[2 * i]).astype(BF16)

    loop(0, half_rows, pick_even)

    @pl.when(y > 0)
    def _():
        halo_row.wait_recv()

    @pl.when(y == 0)
    def _():
        a_s[0, 0] = jnp.zeros_like(a_s[0, 0])

    def windows(r):
        return a_s[r % 2, r // 2 : r // 2 + half_rows].reshape(pix, 3 * mid)

    spre = dot(windows(0), ws[0])
    spre = spre + dot(windows(1), ws[1])
    spre = spre + dot(windows(2), ws[2])
    spre_s[...] = spre
    stk[:, :, 0:mid] = (spre * sigmoid(spre)).astype(BF16).reshape(half_rows, half_cols, mid)

    loop(1, nx, lambda k: weight_x(k).wait_recv())
    weight_core.start()
    weight_core.wait_recv()

    def out_y(k):
        return remote(
            obuf.at[k], out.at[y], y_send_sem.at[8 + k], y_recv_sem.at[8 + k], at_y((y + 4 - k) % 4)
        )

    e_rows = stack_ch // nx

    def expand_block(k):
        owner = (y + 4 - k) % 4
        stacked = stk[...].reshape(pix, stack_ch)
        pre = dot(stacked, wg[k])
        sig = sigmoid(pre)
        value = (pre * sig).astype(BF16)

        @pl.when(k == 0)
        def _():
            out[y] = value

        @pl.when(k > 0)
        def _():
            obuf[k] = value
            out_y(k).start()
            cot_y(k).wait_recv()

        grad = (cotr[k].astype(F32) * slope_of(pre, sig)).astype(BF16)
        term = dot_tn(stacked, grad).astype(BF16)
        for h in range(2):
            for x_at in range(nx):
                e_send[h, x_at * 4 + owner] = term[x_at * e_rows : (x_at + 1) * e_rows, h * lanes : (h + 1) * lanes]
        back = dot_nt(grad, wg[k])

        @pl.when(k == 0)
        def _():
            stg[...] = back

        @pl.when(k > 0)
        def _():
            stg[...] += back

    loop(0, 4, expand_block)

    def core_sum(send, got, k):
        return remote(send.at[1 - core], got, c_send_sem.at[k], c_recv_sem.at[k], other_core)

    def plane_sum(summed, got, group, k):
        slot = group * planes + k
        place = (plane + k) % planes
        return remote(
            summed.at[place], got.at[k], p_send_sem.at[slot], p_recv_sem.at[slot], at_plane(place)
        )

    def add_core(send, got, summed):
        def one(q):
            summed[q] = (send[core, q].astype(F32) + got[q].astype(F32)).astype(BF16)

        loop(0, planes, one)

    def plane_total(summed, got, group):
        def one(k, total):
            plane_sum(summed, got, group, k).wait_recv()
            return total + got[k].astype(F32)

        return lax.fori_loop(1, planes, one, summed[plane].astype(F32))

    e_core = core_sum(e_send, e_rc, 1)
    e_core.start()

    spre = spre_s[...]
    sig = sigmoid(spre)
    sgrad_pre = stg[:, 0:mid] * slope_of(spre, sig)
    sgp[0:half_rows] = sgrad_pre.astype(BF16).reshape(half_rows, half_cols, mid)
    halo_grad = remote(sgp.at[0], sgp.at[half_rows], y_send_sem.at[13], y_recv_sem.at[13], at_y((y + 3) % 4))

    @pl.when(y > 0)
    def _():
        halo_grad.start()

    s_rows = mid * 3 // planes
    flat = sgp[0:half_rows].reshape(pix, mid)
    for r in range(3):
        term = dot_tn(windows(r), flat).astype(BF16)
        for h in range(2):
            for q in range(planes):
                s_send[h, q, r * s_rows : (r + 1) * s_rows] = term[
                    q * s_rows : (q + 1) * s_rows, h * lanes : (h + 1) * lanes
                ]
    s_core = core_sum(s_send, s_rc, 2)
    s_core.start()
    e_core.wait_recv()
    add_core(e_send, e_rc, e_p)
    loop(1, planes, lambda k: plane_sum(e_p, e_rp, 0, k).start())

    @pl.when(y < 3)
    def _():
        halo_grad.wait_recv()

    @pl.when(y == 3)
    def _():
        sgp[half_rows] = jnp.zeros_like(sgp[half_rows])

    sbuf[half_cols : half_cols + 8] = jnp.zeros((8, mid), F32)

    def shift_row(i):
        sbuf[0:half_cols] = sgp[i].astype(F32)
        sgq[i] = sbuf[1 : 1 + half_cols].astype(BF16)

    loop(0, half_rows + 1, shift_row)
    here = sgp[0:half_rows].reshape(pix, mid)
    here_next = sgq[0:half_rows].reshape(pix, mid)

    def weave(row_par, col_par, value):
        value = value.reshape(half_rows, half_cols, mid)
        for i in range(half_rows):
            for block in range(mid // lanes):
                rg_s[2 * i + row_par, block, pl.ds(col_par, half_cols, stride=2), :] = value[
                    i, :, block * lanes : (block + 1) * lanes
                ]

    def tap(r, c):
        return ws[r, c * mid : (c + 1) * mid, :]

    weave(0, 0, dot_nt(here, tap(1, 1)))
    weave(0, 1, dot_nt(here, tap(1, 2)) + dot_nt(here_next, tap(1, 0)))
    below = sgp[1 : half_rows + 1].reshape(pix, mid)
    below_next = sgq[1 : half_rows + 1].reshape(pix, mid)
    weave(1, 0, dot_nt(here, tap(2, 1)) + dot_nt(below, tap(0, 1)))
    weave(
        1, 1,
        dot_nt(here, tap(2, 2)) + dot_nt(here_next, tap(2, 0)) + dot_nt(below, tap(0, 2)) + dot_nt(below_next, tap(0, 0)),
    )
    s_core.wait_recv()
    add_core(s_send, s_rc, s_p)
    loop(1, planes, lambda k: plane_sum(s_p, s_rp, 1, k).start())

    rterm[...] = jnp.zeros_like(rterm)

    def reduce_back(p):
        pre = pre_s[p]
        canvas = jnp.concatenate([rg_s[p, block] for block in range(mid // lanes)], axis=1)
        grad = (canvas * slope_of(pre, sigmoid(pre))).astype(BF16)
        rgp_s[p] = grad
        rterm[...] += dot_tn(img[p], grad)

    loop(0, rows, reduce_back)
    r_rows = chans // planes
    for h in range(2):
        for q in range(planes):
            r_send[h, q] = rterm[q * r_rows : (q + 1) * r_rows, h * lanes : (h + 1) * lanes].astype(BF16)
    r_core = core_sum(r_send, r_rc, 3)
    r_core.start()

    e_z[...] = plane_total(e_p, e_rp, 0).reshape(e_z.shape)

    def z_sum(src, dst, group, k):
        slot = group * nz + k
        return remote(
            src.at[(z + k) % nz], dst.at[k], z_send_sem.at[slot], z_recv_sem.at[slot], at_z((z + k) % nz)
        )

    def z_spread(src, dst, group, k):
        slot = group * nz + k
        return remote(src, dst.at[z], z_send_sem.at[slot], z_recv_sem.at[slot], at_z((z + k) % nz))

    def z_total(src, dst, group):
        def one(k, total):
            z_sum(src, dst, group, k).wait_recv()
            return total + dst[k]

        return lax.fori_loop(1, nz, one, src[z])

    loop(1, nz, lambda k: z_sum(e_z, e_rz, 0, k).start())

    r_core.wait_recv()
    add_core(r_send, r_rc, r_p)
    loop(1, planes, lambda k: plane_sum(r_p, r_rp, 2, k).start())

    e_f[...] = z_total(e_z, e_rz, 0)
    loop(1, nz, lambda k: z_spread(e_f, e_g, 1, k).start())

    def input_row(p):
        wide = dot_nt(rgp_s[p], wr[...])

        @pl.when(p % 2 == 1)
        def _():
            igrad[p] = wide.astype(BF16)

        @pl.when(p % 2 == 0)
        def _():
            first = pl.ds(pl.multiple_of((p // 2) * half_cols, half_cols), half_cols)
            for block in range(chans // lanes):
                lane = slice(block * lanes, (block + 1) * lanes)
                widebuf[block] = wide[:, lane]
                widebuf[block, pl.ds(0, half_cols, stride=2), :] = (
                    widebuf[block, pl.ds(0, half_cols, stride=2), :]
                    + stg[first, mid + block * lanes : mid + (block + 1) * lanes]
                )
                igrad[p, :, lane] = widebuf[block].astype(BF16)

    loop(0, rows, input_row)

    st_rows, rt_rows, t_rows = 3 * s_rows, r_rows, t_z.shape[0] * t_z.shape[1]
    total = [plane_total(s_p, s_rp, 1), plane_total(r_p, r_rp, 2)]
    if t_rows > st_rows + rt_rows:
        total.append(jnp.zeros((t_rows - st_rows - rt_rows, lanes), F32))
    t_z[...] = jnp.concatenate(total, axis=0).reshape(t_z.shape)
    loop(1, nz, lambda k: z_sum(t_z, t_rz, 2, k).start())

    loop(1, nz, lambda k: z_spread(e_f, e_g, 1, k).wait_recv())
    e_g[z] = e_f[...]
    e_out[core, x] = e_g[...].reshape(e_rows, lanes).astype(BF16)

    def e_x(k):
        return remote(
            e_out.at[core, x], e_out.at[core, x], p_send_sem.at[3 * planes + k], p_recv_sem.at[3 * planes + k], at_x((x + k) % nx)
        )

    loop(1, nx, lambda k: e_x(k).start())

    t_f[...] = z_total(t_z, t_rz, 2)
    loop(1, nz, lambda k: z_spread(t_f, t_g, 4, k).start())
    loop(1, nx, lambda k: e_x(k).wait_recv())
    e_cross = remote(e_out.at[core], e_out.at[core], c_send_sem.at[4], c_recv_sem.at[4], other_core)
    loop(1, nx, lambda k: e_x(k).wait_send())
    e_cross.start()

    loop(1, nz, lambda k: z_spread(t_f, t_g, 4, k).wait_recv())
    t_g[z] = t_f[...]
    t_out[core, plane] = t_g[...].reshape(t_rows, lanes).astype(BF16)

    def t_spread(k):
        slot = 4 * planes + k
        return remote(
            t_out.at[core, plane], t_out.at[core, plane], p_send_sem.at[slot], p_recv_sem.at[slot], at_plane((plane + k) % planes)
        )

    def t_cross(k):
        place = (plane + planes - k) % planes
        return remote(
            t_out.at[core, place], t_out.at[core, place], c_send_sem.at[5 + k], c_recv_sem.at[5 + k], other_core
        )

    loop(1, planes, lambda k: t_spread(k).start())
    t_cross(0).start()

    def pass_on(k):
        t_spread(k).wait_recv()
        t_cross(k).start()

    loop(1, planes, pass_on)
    e_cross.wait_recv()
    for h in range(2):
        for x_at in range(nx):
            egrad[x_at * e_rows : (x_at + 1) * e_rows, h * lanes : (h + 1) * lanes] = e_out[h, x_at].astype(F32) * scale
    loop(0, planes, lambda k: t_cross(k).wait_recv())
    for h in range(2):
        lane = slice(h * lanes, (h + 1) * lanes)
        for q in range(planes):
            for r in range(3):
                sgrad[r, q * s_rows : (q + 1) * s_rows, lane] = t_out[h, q, r * s_rows : (r + 1) * s_rows].astype(F32) * scale
            rgrad[q * r_rows : (q + 1) * r_rows, lane] = t_out[h, q, st_rows : st_rows + r_rows].astype(F32) * scale

    @pl.when(y < 3)
    def _():
        halo_row.wait_send()

    @pl.when(y > 0)
    def _():
        halo_grad.wait_send()

    def finish_y(k):
        weight_y(k).wait_send()
        cot_y(k).wait_send()
        out_y(k).wait()

    loop(1, 4, finish_y)
    loop(1, nx, lambda k: weight_x(k).wait_send())
    for copy in (weight_core, e_core, s_core, r_core, e_cross):
        copy.wait_send()

    def finish_plane(k):
        plane_sum(e_p, e_rp, 0, k).wait_send()
        plane_sum(s_p, s_rp, 1, k).wait_send()
        plane_sum(r_p, r_rp, 2, k).wait_send()
        t_spread(k).wait_send()

    loop(1, planes, finish_plane)

    def finish_z(k):
        z_sum(e_z, e_rz, 0, k).wait_send()
        z_spread(e_f, e_g, 1, k).wait_send()
        z_sum(t_z, t_rz, 2, k).wait_send()
        z_spread(t_f, t_g, 4, k).wait_send()

    loop(1, nz, finish_z)
    loop(0, planes, lambda k: t_cross(k).wait_send())


def body(nx, nz, images, reduce_weight, spatial_weight, expand_weight, cotangent):
    image = images[0]
    rows, cols, chans = image.shape
    mid = reduce_weight.shape[1]
    stack_ch, filt = expand_weight.shape
    half_rows, half_cols = rows // 2, cols // 2
    pix = half_rows * half_cols
    planes = nx * 4
    lanes = 128
    e_rows = stack_ch // nx
    s_rows = 9 * mid // planes
    r_rows = chans // planes
    t_rows = -(-(s_rows + r_rows) // (8 * nz)) * 8 * nz
    cot_blocks = cotangent[0].reshape(4, pix, filt)
    weights = spatial_weight.reshape(3, 3 * mid, mid)
    vmem = pl.BlockSpec(memory_space=pltpu.VMEM)
    V = pltpu.VMEM
    D = pltpu.SemaphoreType.DMA
    scratch = [
        V((4, stack_ch, filt), BF16),
        V((4, pix, filt), BF16),
        V((2, half_rows + 1, half_cols, 3 * mid), BF16),
        V((rows, cols, mid), F32),
        V((mid // lanes, cols + 16, lanes), F32),
        V((pix, mid), F32),
        V((half_rows, half_cols, stack_ch), BF16),
        V((4, pix, filt), BF16),
        V((pix, stack_ch), F32),
        V((half_rows + 1, half_cols, mid), BF16),
        V((half_rows + 1, half_cols, mid), BF16),
        V((half_cols + 8, mid), F32),
        V((rows, mid // lanes, cols, lanes), F32),
        V((rows, cols, mid), BF16),
        V((chans, mid), F32),
        V((chans // lanes, cols, lanes), F32),
        V((2, planes, e_rows, lanes), BF16),
        V((planes, e_rows, lanes), BF16),
        V((planes, e_rows, lanes), BF16),
        V((planes, e_rows, lanes), BF16),
        V((nz, e_rows // nz, lanes), F32),
        V((nz, e_rows // nz, lanes), F32),
        V((e_rows // nz, lanes), F32),
        V((nz, e_rows // nz, lanes), F32),
        V((2, nx, e_rows, lanes), BF16),
        V((2, planes, s_rows, lanes), BF16),
        V((planes, s_rows, lanes), BF16),
        V((planes, s_rows, lanes), BF16),
        V((planes, s_rows, lanes), BF16),
        V((2, planes, r_rows, lanes), BF16),
        V((planes, r_rows, lanes), BF16),
        V((planes, r_rows, lanes), BF16),
        V((planes, r_rows, lanes), BF16),
        V((nz, t_rows // nz, lanes), F32),
        V((nz, t_rows // nz, lanes), F32),
        V((t_rows // nz, lanes), F32),
        V((nz, t_rows // nz, lanes), F32),
        V((2, planes, t_rows, lanes), BF16),
        D((14,)),
        D((14,)),
        D((5 * planes,)),
        D((5 * planes,)),
        D((5 * nz,)),
        D((5 * nz,)),
        D((5 + planes,)),
        D((5 + planes,)),
    ]
    output, input_grad, reduce_grad, spatial_grad, expand_grad = pl.pallas_call(
        functools.partial(block_kernel, nx, nz),
        out_shape=(
            jax.ShapeDtypeStruct((4, pix, filt), BF16),
            jax.ShapeDtypeStruct(image.shape, BF16),
            jax.ShapeDtypeStruct((chans, mid), F32),
            jax.ShapeDtypeStruct((3, 3 * mid, mid), F32),
            jax.ShapeDtypeStruct((stack_ch, filt), F32),
        ),
        in_specs=[vmem] * 5,
        out_specs=[vmem] * 5,
        scratch_shapes=scratch,
        compiler_params=pltpu.CompilerParams(
            collective_id=0, has_side_effects=True, vmem_limit_bytes=56 * 1024 * 1024
        ),
    )(image, reduce_weight, weights, expand_weight, cot_blocks)
    return (
        output.reshape((1, 4 * half_rows, half_cols, filt)),
        input_grad[None],
        reduce_grad,
        spatial_grad.reshape(3, 3, mid, mid),
        expand_grad,
    )


def solution(mesh):
    nx = 4 if mesh.shape["dp"] >= 32 else 2
    nz = mesh.shape["dp"] // (2 * nx)
    return jax.shard_map(
        functools.partial(body, nx, nz),
        mesh=mesh,
        in_specs=(
            P("dp", ("space", "chan"), None, None),
            P(),
            P(),
            P(None, ("space", "chan")),
            P("dp", None, None, ("space", "chan")),
        ),
        out_specs=(
            P("dp", None, None, ("space", "chan")),
            P("dp", ("space", "chan"), None, None),
            P(),
            P(),
            P(None, ("space", "chan")),
        ),
        check_vma=False,
    )
```

time: 638 us -> 107 us (0.17)
  waiting for transfers between devices: 527 us -> 0 us
  Pallas kernels: 0 us -> 98 us
  matrix products: 36.5 us -> 0 us
  local copies, waits for them, and re-layouts: 41 us -> 7.78 us
  between operations: 14.3 us -> 0.65 us
  other arithmetic: 12.2 us -> 0 us
    psum x2 -> x0, waiting for transfers between devices: 419 us -> none  [the longest x1 263 us: body(): lax.psum((reduce_term, spatial_term), ('dp', 'space', 'chan'))]
    pallas_call x0 -> x1, Pallas kernels: none -> 98 us  [body(): pl.pallas_call(functools.partial(block_kernel, nx, nz), out_shape=(jax.Sh...]
    reduce_scatter x1 -> x0, waiting for transfers between devices: 62.3 us -> none  [body(): lax.psum_scatter(jnp.dot(grad_pre, expand_weight.T, preferred_element_typ...]
    all_gather x1 -> x0, waiting for transfers between devices: 45.2 us -> none  [body(): stacked_all = lax.all_gather(stacked, ('space', 'chan'), axis=0, tiled=True)]
    dot_general x30 -> x0, matrix products: 35.7 us -> none  [the longest x9 9.73 us: body(): jnp.dot(window.reshape(-1, middle).T, flat_spatial, preferred_element_typ...]
    slice x16 -> x0, local copies, waits for them, and re-layouts: 28.9 us -> none  [the longest x9 19.9 us: taps(): padded[row_off:row_off + rows:2, col_off:col_off + cols:2]]
    mul x3 -> x0, other arithmetic: 6.5 us -> none  [the longest x1 3.32 us: body(): spatial_total * scale]
  transfers between devices with their start and end apart: 6 -> 0, of which waited for: 4 -> 0; matrix products, arithmetic and copies ran while one was open for 7% -> 0% of each run, Pallas kernels for 0% -> 0%
where the time goes in v1:
time: 107 us; the launch traced here: 106 us
  Pallas kernels  98 us (92%)
  local copies, waits for them, and re-layouts  7.78 us (7%)
    pallas_call x1, Pallas kernels, body(): pl.pallas_call(functools.partial(block_kernel, nx, nz), out_shape=(jax.Sh...  98 us
    unnamed x13, local copies, waits for them, and re-layouts  7.78 us

profile of v1, /device:TPU:1, one launch (start us, length us, event | category | flops | bytes accessed | tf_op | source)
XLA Modules:
  0.0 106.4 jit_solution(2876425622607679730)
XLA Ops:
  0.6 98.0 %shard_map.92 = (bf16[4,512,256]{2,1,0:T(8,128)(2,1)}, bf16[8,256,512]{2,1,0:T(8,128)(2,1)}, f32[512,256]{1,0:T(8,128)}, f32[3,768,256]{2,1,0:T(8,128)}, f32[768,256]{1,0:T(8,128)}) custom-call(bf16[8,256,512]{2,1,0:T(8,128)(2,1)} %bitcast.7, bf16[512,256]{1,0:T(8,128)(2,1)} %wr.1, bf16[3,768,256]{2,1,0:T(8,128)(2,1)} %bitcast.9, bf16[768,256]{1,0:T(8,128)(2,1)} %we.1, ...), custom_call_target="tpu_custom_call" | custom-call | tf_op jit(solution)/shard_map/pallas_call | solution.py:549
  98.6 0.0 copy-start.1
  98.6 2.4 %copy.15 = bf16[1,16,128,256]{3,2,1,0:T(8,128)(2,1)} copy(bf16[1,16,128,256]{3,2,1,0:T(8,128)(2,1)} %bitcast.11) | data formatting | bytes 2097152
  101.1 0.0 copy-done.1
  101.1 0.0 copy-start.3
  101.1 0.0 copy-start
  101.1 1.3 %copy.16 = bf16[1,8,256,512]{3,2,1,0:T(8,128)(2,1)} copy(bf16[1,8,256,512]{3,2,1,0:T(8,128)(2,1)S(1)} %bitcast.8) | data formatting | bytes 4194304
  102.4 0.1 copy-done.3
  102.4 0.8 copy.17
  103.2 0.6 copy-done
  103.8 0.0 copy-start.2
  103.8 1.4 %copy.18 = f32[3,3,256,256]{3,2,1,0:T(8,128)} copy(f32[3,3,256,256]{3,2,1,0:T(8,128)S(1)} %bitcast.6) | data formatting | bytes 4718592
  105.3 0.3 copy-done.2
  105.5 0.9 copy.19
Async XLA Ops:
  98.6 2.4 %copy-start.1 = (bf16[8,256,512]{2,1,0:T(8,128)(2,1)S(1)}, bf16[8,256,512]{2,1,0:T(8,128)(2,1)}, u32[]{:S(2)}) copy-start(bf16[8,256,512]{2,1,0:T(8,128)(2,1)} %get-tuple-element.11) | copy-start | bytes 6291460
  101.1 1.4 %copy-start.3 = (f32[512,256]{1,0:T(8,128)S(1)}, f32[512,256]{1,0:T(8,128)}, u32[]{:S(2)}) copy-start(f32[512,256]{1,0:T(8,128)} %get-tuple-element.22) | copy-start | bytes 1572868
  101.1 2.8 %copy-start = (f32[3,768,256]{2,1,0:T(8,128)S(1)}, f32[3,768,256]{2,1,0:T(8,128)}, u32[]{:S(2)}) copy-start(f32[3,768,256]{2,1,0:T(8,128)} %get-tuple-element.13) | copy-start | bytes 7077892
  103.8 1.7 %copy-start.2 = (f32[768,256]{1,0:T(8,128)S(1)}, f32[768,256]{1,0:T(8,128)}, u32[]{:S(2)}) copy-start(f32[768,256]{1,0:T(8,128)} %get-tuple-element.24) | copy-start | bytes 2359300

commit v2 on v1

--- a/solution.py
+++ b/solution.py
@@ -42,12 +42,12 @@
 
 
 def block_kernel(
-    nx, nz, img, wr, ws, we, cot,
+    nx, nz, img_hbm, wr_hbm, ws_hbm, we, cot,
     out, igrad, rgrad, sgrad, egrad,
-    wg, cotr, a_s, pre_s, rowbuf, spre_s, stk, obuf, stg, sgp, sgq, sbuf, rg_s, rgp_s, rterm, widebuf,
+    img, wr, ws, slp, wg, cotr, a_s, pre_s, rowbuf, spre_s, stk, obuf, stg, sgp, sgq, sbuf, rg_s, rgp_s, rterm, widebuf,
     e_send, e_rc, e_p, e_rp, e_z, e_rz, e_f, e_g, e_out,
     s_send, s_rc, s_p, s_rp, r_send, r_rc, r_p, r_rp, t_z, t_rz, t_f, t_g, t_out,
-    y_send_sem, y_recv_sem, p_send_sem, p_recv_sem, z_send_sem, z_recv_sem, c_send_sem, c_recv_sem,
+    y_send_sem, y_recv_sem, p_send_sem, p_recv_sem, z_send_sem, z_recv_sem, c_send_sem, c_recv_sem, w_send_sem, w_recv_sem, load_sem,
 ):
     rows, cols, chans = img.shape
     half_cols = cols // 2
@@ -99,9 +99,24 @@
     loop(1, planes, greet_plane)
     loop(1, nz, greet_z)
 
+    load_wr = pltpu.make_async_copy(wr_hbm, wr, load_sem.at[rows])
+    load_ws = pltpu.make_async_copy(ws_hbm, ws, load_sem.at[rows + 1])
+    load_we = pltpu.make_async_copy(we, wg.at[0], load_sem.at[rows + 2])
+    load_cot = pltpu.make_async_copy(cot.at[y], cotr.at[0], load_sem.at[rows + 3])
+
+    def load_row(p):
+        return pltpu.make_async_copy(img_hbm.at[p], img.at[p], load_sem.at[p])
+
+    load_wr.start()
+    loop(0, rows, lambda p: load_row(p).start())
+    load_ws.start()
+    load_we.start()
+    load_cot.start()
+
     rowbuf[:, 0:8] = jnp.zeros((mid // lanes, 8, lanes), F32)
 
     def reduce_row(p):
+        load_row(p).wait()
         pre = dot(img[p], wr[...])
         pre_s[p] = pre
         reduced = pre * sigmoid(pre)
@@ -112,16 +127,9 @@
                 lane = part * mid + block * lanes
                 a_s[a_par, a_idx, :, lane : lane + lanes] = rowbuf[block, pl.ds(start, half_cols, stride=2), :].astype(BF16)
 
-    reduce_row(rows - 1)
+    load_wr.wait()
+    loop(0, rows, reduce_row)
     pl.semaphore_wait(barrier, planes + nz - 1)
-
-    halo_row = remote(
-        a_s.at[0, half_rows], a_s.at[0, 0], y_send_sem.at[12], y_recv_sem.at[12], at_y((y + 1) % 4)
-    )
-
-    @pl.when(y < 3)
-    def _():
-        halo_row.start()
 
     part_rows = stack_ch // (2 * nx)
     part = pl.ds(pl.multiple_of((core * nx + x) * part_rows, part_rows), part_rows)
@@ -130,27 +138,33 @@
     def weight_y(k):
         return remote(we.at[part], wg.at[k, part], y_send_sem.at[k], y_recv_sem.at[k], at_y((y + k) % 4))
 
-    def weight_x(k):
-        return remote(
-            wg.at[1:4, part], wg.at[1:4, part], z_send_sem.at[3 * nz + k], z_recv_sem.at[3 * nz + k], at_x((x + k) % nx)
-        )
-
-    weight_core = remote(wg.at[1:4, half_part], wg.at[1:4, half_part], c_send_sem.at[0], c_recv_sem.at[0], other_core)
+    def weight_x(k, j):
+        slot = k * nx + j
+        return remote(wg.at[k, part], wg.at[k, part], w_send_sem.at[slot], w_recv_sem.at[slot], at_x((x + j) % nx))
+
+    def weight_core(k):
+        return remote(wg.at[k, half_part], wg.at[k, half_part], c_send_sem.at[k], c_recv_sem.at[k], other_core)
 
     def cot_y(k):
         return remote(
             cot.at[(y + k) % 4], cotr.at[k], y_send_sem.at[4 + k], y_recv_sem.at[4 + k], at_y((y + k) % 4)
         )
 
-    loop(1, 4, lambda k: weight_y(k).start())
-    loop(1, 4, lambda k: cot_y(k).start())
-
-    wg[0] = we[...]
-    cotr[0] = cot[y]
-    loop(0, 2, reduce_row)
-    loop(1, 4, lambda k: weight_y(k).wait_recv())
-    loop(1, nx, lambda k: weight_x(k).start())
-    loop(2, rows - 1, reduce_row)
+    def halo_part(index):
+        return a_s.at[0, index, :, mid : 3 * mid]
+
+    halo_row = remote(
+        halo_part(half_rows), halo_part(0), y_send_sem.at[12], y_recv_sem.at[12], at_y((y + 1) % 4)
+    )
+    for k in (1, 3, 2):
+        weight_y(k).start()
+
+    @pl.when(y < 3)
+    def _():
+        halo_row.start()
+
+    for k in (1, 3, 2):
+        cot_y(k).start()
 
     take = (
         lax.broadcasted_iota(jnp.int32, (half_cols, cols), 1)
@@ -162,67 +176,85 @@
 
     loop(0, half_rows, pick_even)
 
-    @pl.when(y > 0)
-    def _():
-        halo_row.wait_recv()
-
-    @pl.when(y == 0)
-    def _():
-        a_s[0, 0] = jnp.zeros_like(a_s[0, 0])
-
     def windows(r):
         return a_s[r % 2, r // 2 : r // 2 + half_rows].reshape(pix, 3 * mid)
 
-    spre = dot(windows(0), ws[0])
-    spre = spre + dot(windows(1), ws[1])
-    spre = spre + dot(windows(2), ws[2])
+    load_ws.wait()
+    spre_s[...] = dot(windows(1), ws[1]) + dot(windows(2), ws[2])
+    for k in (1, 3, 2):
+        weight_y(k).wait_recv()
+        loop(1, nx, lambda j: weight_x(k, j).start())
+
+    @pl.when(y > 0)
+    def _():
+        halo_row.wait_recv()
+        sbuf[0:8] = jnp.zeros((8, mid), F32)
+        sbuf[8 : 8 + half_cols] = a_s[0, 0, :, 2 * mid : 3 * mid].astype(F32)
+        a_s[0, 0, :, 0:mid] = sbuf[7 : 7 + half_cols].astype(BF16)
+
+    @pl.when(y == 0)
+    def _():
+        a_s[0, 0] = jnp.zeros_like(a_s[0, 0])
+
+    spre = spre_s[...] + dot(windows(0), ws[0])
     spre_s[...] = spre
     stk[:, :, 0:mid] = (spre * sigmoid(spre)).astype(BF16).reshape(half_rows, half_cols, mid)
 
-    loop(1, nx, lambda k: weight_x(k).wait_recv())
-    weight_core.start()
-    weight_core.wait_recv()
-
     def out_y(k):
         return remote(
             obuf.at[k], out.at[y], y_send_sem.at[8 + k], y_recv_sem.at[8 + k], at_y((y + 4 - k) % 4)
         )
 
-    e_rows = stack_ch // nx
-
     def expand_block(k):
-        owner = (y + 4 - k) % 4
-        stacked = stk[...].reshape(pix, stack_ch)
-        pre = dot(stacked, wg[k])
+        pre = dot(stk[...].reshape(pix, stack_ch), wg[k])
         sig = sigmoid(pre)
         value = (pre * sig).astype(BF16)
-
-        @pl.when(k == 0)
-        def _():
+        slp[k] = slope_of(pre, sig)
+        if k == 0:
             out[y] = value
-
-        @pl.when(k > 0)
-        def _():
+        else:
             obuf[k] = value
-            out_y(k).start()
-            cot_y(k).wait_recv()
-
-        grad = (cotr[k].astype(F32) * slope_of(pre, sig)).astype(BF16)
-        term = dot_tn(stacked, grad).astype(BF16)
+
+    def weight_relay(k):
+        loop(1, nx, lambda j: weight_x(k, j).wait_recv())
+        weight_core(k).start()
+
+    e_rows = stack_ch // nz
+
+    def expand_back(k):
+        owner = (y + 4 - k) % 4
+        grad = (cotr[k].astype(F32) * slp[k]).astype(BF16)
+        term = dot_tn(stk[...].reshape(pix, stack_ch), grad).astype(BF16)
         for h in range(2):
-            for x_at in range(nx):
-                e_send[h, x_at * 4 + owner] = term[x_at * e_rows : (x_at + 1) * e_rows, h * lanes : (h + 1) * lanes]
+            for z_at in range(nz):
+                e_send[h, z_at, owner] = term[z_at * e_rows : (z_at + 1) * e_rows, h * lanes : (h + 1) * lanes]
         back = dot_nt(grad, wg[k])
-
-        @pl.when(k == 0)
-        def _():
+        if k == 0:
             stg[...] = back
-
-        @pl.when(k > 0)
-        def _():
+        else:
             stg[...] += back
 
-    loop(0, 4, expand_block)
+    load_we.wait()
+    load_cot.wait()
+    expand_block(0)
+    weight_relay(1)
+    expand_back(0)
+    weight_relay(3)
+    weight_core(1).wait_recv()
+    expand_block(1)
+    weight_relay(2)
+    weight_core(3).wait_recv()
+    expand_block(3)
+    cot_y(1).wait_recv()
+    expand_back(1)
+    weight_core(2).wait_recv()
+    expand_block(2)
+    cot_y(3).wait_recv()
+    expand_back(3)
+    cot_y(2).wait_recv()
+    out_y(1).start()
+    out_y(3).start()
+    expand_back(2)
 
     def core_sum(send, got, k):
         return remote(send.at[1 - core], got, c_send_sem.at[k], c_recv_sem.at[k], other_core)
@@ -238,7 +270,7 @@
         def one(q):
             summed[q] = (send[core, q].astype(F32) + got[q].astype(F32)).astype(BF16)
 
-        loop(0, planes, one)
+        loop(0, summed.shape[0], one)
 
     def plane_total(summed, got, group):
         def one(k, total):
@@ -247,7 +279,24 @@
 
         return lax.fori_loop(1, planes, one, summed[plane].astype(F32))
 
-    e_core = core_sum(e_send, e_rc, 1)
+    def z_sum(src, dst, group, k):
+        slot = group * nz + k
+        return remote(
+            src.at[(z + k) % nz], dst.at[k], z_send_sem.at[slot], z_recv_sem.at[slot], at_z((z + k) % nz)
+        )
+
+    def z_spread(src, dst, group, k):
+        slot = group * nz + k
+        return remote(src, dst.at[z], z_send_sem.at[slot], z_recv_sem.at[slot], at_z((z + k) % nz))
+
+    def z_total(src, dst, group):
+        def one(k, total):
+            z_sum(src, dst, group, k).wait_recv()
+            return total + dst[k].astype(F32)
+
+        return lax.fori_loop(1, nz, one, src[z].astype(F32))
+
+    e_core = core_sum(e_send, e_rc, 4)
     e_core.start()
 
     spre = spre_s[...]
@@ -269,11 +318,14 @@
                 s_send[h, q, r * s_rows : (r + 1) * s_rows] = term[
                     q * s_rows : (q + 1) * s_rows, h * lanes : (h + 1) * lanes
                 ]
-    s_core = core_sum(s_send, s_rc, 2)
+    s_core = core_sum(s_send, s_rc, 5)
     s_core.start()
     e_core.wait_recv()
     add_core(e_send, e_rc, e_p)
-    loop(1, planes, lambda k: plane_sum(e_p, e_rp, 0, k).start())
+    loop(1, nz, lambda k: z_sum(e_p, e_rp, 0, k).start())
+    s_core.wait_recv()
+    add_core(s_send, s_rc, s_p)
+    loop(1, planes, lambda k: plane_sum(s_p, s_rp, 1, k).start())
 
     @pl.when(y < 3)
     def _():
@@ -313,10 +365,6 @@
         1, 1,
         dot_nt(here, tap(2, 2)) + dot_nt(here_next, tap(2, 0)) + dot_nt(below, tap(0, 2)) + dot_nt(below_next, tap(0, 0)),
     )
-    s_core.wait_recv()
-    add_core(s_send, s_rc, s_p)
-    loop(1, planes, lambda k: plane_sum(s_p, s_rp, 1, k).start())
-
     rterm[...] = jnp.zeros_like(rterm)
 
     def reduce_back(p):
@@ -331,36 +379,13 @@
     for h in range(2):
         for q in range(planes):
             r_send[h, q] = rterm[q * r_rows : (q + 1) * r_rows, h * lanes : (h + 1) * lanes].astype(BF16)
-    r_core = core_sum(r_send, r_rc, 3)
+    r_core = core_sum(r_send, r_rc, 6)
     r_core.start()
 
-    e_z[...] = plane_total(e_p, e_rp, 0).reshape(e_z.shape)
-
-    def z_sum(src, dst, group, k):
-        slot = group * nz + k
-        return remote(
-            src.at[(z + k) % nz], dst.at[k], z_send_sem.at[slot], z_recv_sem.at[slot], at_z((z + k) % nz)
-        )
-
-    def z_spread(src, dst, group, k):
-        slot = group * nz + k
-        return remote(src, dst.at[z], z_send_sem.at[slot], z_recv_sem.at[slot], at_z((z + k) % nz))
-
-    def z_total(src, dst, group):
-        def one(k, total):
-            z_sum(src, dst, group, k).wait_recv()
-            return total + dst[k]
-
-        return lax.fori_loop(1, nz, one, src[z])
-
-    loop(1, nz, lambda k: z_sum(e_z, e_rz, 0, k).start())
-
+    out_y(2).start()
     r_core.wait_recv()
     add_core(r_send, r_rc, r_p)
     loop(1, planes, lambda k: plane_sum(r_p, r_rp, 2, k).start())
-
-    e_f[...] = z_total(e_z, e_rz, 0)
-    loop(1, nz, lambda k: z_spread(e_f, e_g, 1, k).start())
 
     def input_row(p):
         wide = dot_nt(rgp_s[p], wr[...])
@@ -390,23 +415,31 @@
     t_z[...] = jnp.concatenate(total, axis=0).reshape(t_z.shape)
     loop(1, nz, lambda k: z_sum(t_z, t_rz, 2, k).start())
 
-    loop(1, nz, lambda k: z_spread(e_f, e_g, 1, k).wait_recv())
-    e_g[z] = e_f[...]
-    e_out[core, x] = e_g[...].reshape(e_rows, lanes).astype(BF16)
-
-    def e_x(k):
-        return remote(
-            e_out.at[core, x], e_out.at[core, x], p_send_sem.at[3 * planes + k], p_recv_sem.at[3 * planes + k], at_x((x + k) % nx)
-        )
-
-    loop(1, nx, lambda k: e_x(k).start())
+    e_z[...] = z_total(e_p, e_rp, 0).reshape(e_z.shape)
+
+    def e_plane(k):
+        place = (plane + k) % planes
+        return remote(
+            e_z.at[place % 4, place // 4], e_rz.at[k], p_send_sem.at[k], p_recv_sem.at[k], at_plane(place)
+        )
+
+    loop(1, planes, lambda k: e_plane(k).start())
 
     t_f[...] = z_total(t_z, t_rz, 2)
     loop(1, nz, lambda k: z_spread(t_f, t_g, 4, k).start())
-    loop(1, nx, lambda k: e_x(k).wait_recv())
-    e_cross = remote(e_out.at[core], e_out.at[core], c_send_sem.at[4], c_recv_sem.at[4], other_core)
-    loop(1, nx, lambda k: e_x(k).wait_send())
-    e_cross.start()
+
+    def e_total(k, total):
+        e_plane(k).wait_recv()
+        return total + e_rz[k]
+
+    e_f[...] = lax.fori_loop(1, planes, e_total, e_z[y, x])
+
+    def e_x(k):
+        return remote(
+            e_f, e_g.at[x], p_send_sem.at[3 * planes + k], p_recv_sem.at[3 * planes + k], at_x((x + k) % nx)
+        )
+
+    loop(1, nx, lambda k: e_x(k).start())
 
     loop(1, nz, lambda k: z_spread(t_f, t_g, 4, k).wait_recv())
     t_g[z] = t_f[...]
@@ -421,28 +454,58 @@
     def t_cross(k):
         place = (plane + planes - k) % planes
         return remote(
-            t_out.at[core, place], t_out.at[core, place], c_send_sem.at[5 + k], c_recv_sem.at[5 + k], other_core
+            t_out.at[core, place], t_out.at[core, place], c_send_sem.at[8 + k], c_recv_sem.at[8 + k], other_core
         )
 
     loop(1, planes, lambda k: t_spread(k).start())
     t_cross(0).start()
+
+    loop(1, nx, lambda k: e_x(k).wait_recv())
+    e_g[x] = e_f[...]
+    e_out[core, z] = e_g[...].reshape(e_rows, lanes).astype(BF16)
+
+    def e_back(k):
+        slot = nz + k
+        return remote(
+            e_out.at[core, z], e_out.at[core, z], z_send_sem.at[slot], z_recv_sem.at[slot], at_z((z + k) % nz)
+        )
+
+    loop(1, nz, lambda k: e_back(k).start())
 
     def pass_on(k):
         t_spread(k).wait_recv()
         t_cross(k).start()
 
     loop(1, planes, pass_on)
+    loop(1, nz, lambda k: e_back(k).wait())
+    e_cross = remote(e_out.at[core], e_out.at[core], c_send_sem.at[7], c_recv_sem.at[7], other_core)
+    e_cross.start()
+
+    def finish_place(h, q):
+        lane = slice(h * lanes, (h + 1) * lanes)
+        for r in range(3):
+            rows_at = pl.ds(pl.multiple_of(q * s_rows, s_rows), s_rows)
+            sgrad[r, rows_at, lane] = t_out[h, q, r * s_rows : (r + 1) * s_rows].astype(F32) * scale
+        rows_at = pl.ds(pl.multiple_of(q * r_rows, r_rows), r_rows)
+        rgrad[rows_at, lane] = t_out[h, q, st_rows : st_rows + r_rows].astype(F32) * scale
+
+    for h in range(2):
+
+        @pl.when(core == h)
+        def _():
+            loop(0, planes, lambda q: finish_place(h, q))
+
+    loop(0, planes, lambda k: t_cross(k).wait_recv())
+    for h in range(2):
+
+        @pl.when(core != h)
+        def _():
+            loop(0, planes, lambda q: finish_place(h, q))
+
     e_cross.wait_recv()
     for h in range(2):
-        for x_at in range(nx):
-            egrad[x_at * e_rows : (x_at + 1) * e_rows, h * lanes : (h + 1) * lanes] = e_out[h, x_at].astype(F32) * scale
-    loop(0, planes, lambda k: t_cross(k).wait_recv())
-    for h in range(2):
-        lane = slice(h * lanes, (h + 1) * lanes)
-        for q in range(planes):
-            for r in range(3):
-                sgrad[r, q * s_rows : (q + 1) * s_rows, lane] = t_out[h, q, r * s_rows : (r + 1) * s_rows].astype(F32) * scale
-            rgrad[q * r_rows : (q + 1) * r_rows, lane] = t_out[h, q, st_rows : st_rows + r_rows].astype(F32) * scale
+        for z_at in range(nz):
+            egrad[z_at * e_rows : (z_at + 1) * e_rows, h * lanes : (h + 1) * lanes] = e_out[h, z_at].astype(F32) * scale
 
     @pl.when(y < 3)
     def _():
@@ -458,12 +521,15 @@
         out_y(k).wait()
 
     loop(1, 4, finish_y)
-    loop(1, nx, lambda k: weight_x(k).wait_send())
-    for copy in (weight_core, e_core, s_core, r_core, e_cross):
+    for k in range(1, 4):
+        loop(1, nx, lambda j: weight_x(k, j).wait_send())
+        weight_core(k).wait_send()
+    for copy in (e_core, s_core, r_core, e_cross):
         copy.wait_send()
+    loop(1, nx, lambda k: e_x(k).wait_send())
 
     def finish_plane(k):
-        plane_sum(e_p, e_rp, 0, k).wait_send()
+        e_plane(k).wait_send()
         plane_sum(s_p, s_rp, 1, k).wait_send()
         plane_sum(r_p, r_rp, 2, k).wait_send()
         t_spread(k).wait_send()
@@ -471,8 +537,7 @@
     loop(1, planes, finish_plane)
 
     def finish_z(k):
-        z_sum(e_z, e_rz, 0, k).wait_send()
-        z_spread(e_f, e_g, 1, k).wait_send()
+        z_sum(e_p, e_rp, 0, k).wait_send()
         z_sum(t_z, t_rz, 2, k).wait_send()
         z_spread(t_f, t_g, 4, k).wait_send()
 
@@ -489,7 +554,8 @@
     pix = half_rows * half_cols
     planes = nx * 4
     lanes = 128
-    e_rows = stack_ch // nx
+    e_rows = stack_ch // nz
+    f_rows = e_rows // nx
     s_rows = 9 * mid // planes
     r_rows = chans // planes
     t_rows = -(-(s_rows + r_rows) // (8 * nz)) * 8 * nz
@@ -499,6 +565,10 @@
     V = pltpu.VMEM
     D = pltpu.SemaphoreType.DMA
     scratch = [
+        V(image.shape, BF16),
+        V(reduce_weight.shape, BF16),
+        V(weights.shape, BF16),
+        V((4, pix, filt), F32),
         V((4, stack_ch, filt), BF16),
         V((4, pix, filt), BF16),
         V((2, half_rows + 1, half_cols, 3 * mid), BF16),
@@ -510,20 +580,20 @@
         V((pix, stack_ch), F32),
         V((half_rows + 1, half_cols, mid), BF16),
         V((half_rows + 1, half_cols, mid), BF16),
-        V((half_cols + 8, mid), F32),
+        V((half_cols + 16, mid), F32),
         V((rows, mid // lanes, cols, lanes), F32),
         V((rows, cols, mid), BF16),
         V((chans, mid), F32),
         V((chans // lanes, cols, lanes), F32),
-        V((2, planes, e_rows, lanes), BF16),
-        V((planes, e_rows, lanes), BF16),
-        V((planes, e_rows, lanes), BF16),
-        V((planes, e_rows, lanes), BF16),
-        V((nz, e_rows // nz, lanes), F32),
-        V((nz, e_rows // nz, lanes), F32),
-        V((e_rows // nz, lanes), F32),
-        V((nz, e_rows // nz, lanes), F32),
-        V((2, nx, e_rows, lanes), BF16),
+        V((2, nz, 4, e_rows, lanes), BF16),
+        V((nz, 4, e_rows, lanes), BF16),
+        V((nz, 4, e_rows, lanes), BF16),
+        V((nz, 4, e_rows, lanes), BF16),
+        V((4, nx, f_rows, lanes), F32),
+        V((planes, f_rows, lanes), F32),
+        V((f_rows, lanes), F32),
+        V((nx, f_rows, lanes), F32),
+        V((2, nz, e_rows, lanes), BF16),
         V((2, planes, s_rows, lanes), BF16),
         V((planes, s_rows, lanes), BF16),
         V((planes, s_rows, lanes), BF16),
@@ -543,23 +613,26 @@
         D((5 * planes,)),
         D((5 * nz,)),
         D((5 * nz,)),
-        D((5 + planes,)),
-        D((5 + planes,)),
+        D((8 + planes,)),
+        D((8 + planes,)),
+        D((4 * nx,)),
+        D((4 * nx,)),
+        D((rows + 4,)),
     ]
     output, input_grad, reduce_grad, spatial_grad, expand_grad = pl.pallas_call(
         functools.partial(block_kernel, nx, nz),
         out_shape=(
-            jax.ShapeDtypeStruct((4, pix, filt), BF16),
-            jax.ShapeDtypeStruct(image.shape, BF16),
-            jax.ShapeDtypeStruct((chans, mid), F32),
-            jax.ShapeDtypeStruct((3, 3 * mid, mid), F32),
-            jax.ShapeDtypeStruct((stack_ch, filt), F32),
+            pltpu.VMEM((4, pix, filt), BF16),
+            pltpu.VMEM(image.shape, BF16),
+            pltpu.VMEM((chans, mid), F32),
+            pltpu.VMEM((3, 3 * mid, mid), F32),
+            pltpu.VMEM((stack_ch, filt), F32),
         ),
-        in_specs=[vmem] * 5,
+        in_specs=[pl.BlockSpec(memory_space=pltpu.HBM)] * 5,
         out_specs=[vmem] * 5,
         scratch_shapes=scratch,
         compiler_params=pltpu.CompilerParams(
-            collective_id=0, has_side_effects=True, vmem_limit_bytes=56 * 1024 * 1024
+            collective_id=0, has_side_effects=True, vmem_limit_bytes=48 * 1024 * 1024
         ),
     )(image, reduce_weight, weights, expand_weight, cot_blocks)
     return (

time: 107 us -> 90.4 us (0.84)
  Pallas kernels: 98 us -> 84.3 us
  local copies, waits for them, and re-layouts: 7.78 us -> 5.37 us
    pallas_call x1, Pallas kernels: 98 us -> 84.3 us  [body(): pl.pallas_call(functools.partial(block_kernel, nx, nz), out_shape=(pltpu....]
    unnamed x13 -> x5, local copies, waits for them, and re-layouts: 7.78 us -> 5.37 us
where the time goes in v2:
time: 90.4 us; the launch traced here: 90.3 us
  Pallas kernels  84.3 us (93%)
  local copies, waits for them, and re-layouts  5.37 us (6%)
    pallas_call x1, Pallas kernels, body(): pl.pallas_call(functools.partial(block_kernel, nx, nz), out_shape=(pltpu....  84.3 us
    unnamed x5, local copies, waits for them, and re-layouts  5.37 us

profile of v2, /device:TPU:1, one launch (start us, length us, event | category | flops | bytes accessed | tf_op | source)
XLA Modules:
  0.0 90.3 jit_solution(16709489459786536960)
XLA Ops:
  0.6 84.3 %shard_map.92 = (bf16[4,512,256]{2,1,0:T(8,128)(2,1)S(1)}, bf16[8,256,512]{2,1,0:T(8,128)(2,1)S(1)}, f32[512,256]{1,0:T(8,128)S(1)}, f32[3,768,256]{2,1,0:T(8,128)S(1)}, f32[768,256]{1,0:T(8,128)S(1)}) custom-call(bf16[8,256,512]{2,1,0:T(8,128)(2,1)} %bitcast.9, bf16[512,256]{1,0:T(8,128)(2,1)} %wr_hbm.1, bf16[3,768,256]{2,1,0:T(8,128)(2,1)} %bitcast.10, ...), custom_call_target="tpu_custom_call" | custom-call | tf_op jit(solution)/shard_map/pallas_call | solution.py:622
  84.9 1.0 %copy.15 = bf16[1,16,128,256]{3,2,1,0:T(8,128)(2,1)} copy(bf16[1,16,128,256]{3,2,1,0:T(8,128)(2,1)S(1)} %bitcast.8) | data formatting | bytes 2097152
  85.9 1.3 %copy.16 = bf16[1,8,256,512]{3,2,1,0:T(8,128)(2,1)} copy(bf16[1,8,256,512]{3,2,1,0:T(8,128)(2,1)S(1)} %bitcast.7) | data formatting | bytes 4194304
  87.2 0.8 copy.17
  88.0 0.9 copy.19
  88.9 1.4 %copy.18 = f32[3,3,256,256]{3,2,1,0:T(8,128)} copy(f32[3,3,256,256]{3,2,1,0:T(8,128)S(1)} %bitcast.6) | data formatting | bytes 4718592

commit v3 on v2

--- a/solution.py
+++ b/solution.py
@@ -46,8 +46,8 @@
     out, igrad, rgrad, sgrad, egrad,
     img, wr, ws, slp, wg, cotr, a_s, pre_s, rowbuf, spre_s, stk, obuf, stg, sgp, sgq, sbuf, rg_s, rgp_s, rterm, widebuf,
     e_send, e_rc, e_p, e_rp, e_z, e_rz, e_f, e_g, e_out,
-    s_send, s_rc, s_p, s_rp, r_send, r_rc, r_p, r_rp, t_z, t_rz, t_f, t_g, t_out,
-    y_send_sem, y_recv_sem, p_send_sem, p_recv_sem, z_send_sem, z_recv_sem, c_send_sem, c_recv_sem, w_send_sem, w_recv_sem, load_sem,
+    s_send, s_rc, s_p, s_a1, s_am, s_a2, s_b1, s_bm, s_b2, r_send, r_rc, r_p, r_rp, t_z, t_rz, t_f, t_g, t_out,
+    y_send_sem, y_recv_sem, p_send_sem, p_recv_sem, z_send_sem, z_recv_sem, c_send_sem, c_recv_sem, w_send_sem, w_recv_sem, e_send_sem, e_recv_sem, q_send_sem, q_recv_sem, load_sem,
 ):
     rows, cols, chans = img.shape
     half_cols = cols // 2
@@ -227,34 +227,63 @@
         term = dot_tn(stk[...].reshape(pix, stack_ch), grad).astype(BF16)
         for h in range(2):
             for z_at in range(nz):
-                e_send[h, z_at, owner] = term[z_at * e_rows : (z_at + 1) * e_rows, h * lanes : (h + 1) * lanes]
+                e_send[h, owner, z_at] = term[z_at * e_rows : (z_at + 1) * e_rows, h * lanes : (h + 1) * lanes]
         back = dot_nt(grad, wg[k])
         if k == 0:
             stg[...] = back
         else:
             stg[...] += back
 
+    def e_owner(k):
+        return (y + 4 - k) % 4
+
+    def e_core(k):
+        owner = e_owner(k)
+        return remote(e_send.at[1 - core, owner], e_rc.at[owner], c_send_sem.at[4 + k], c_recv_sem.at[4 + k], other_core)
+
+    def e_sum(k, j):
+        owner, z_at, slot = e_owner(k), (z + j) % nz, k * nz + j
+        return remote(
+            e_p.at[owner, z_at], e_rp.at[owner, j], e_send_sem.at[slot], e_recv_sem.at[slot], at_z(z_at)
+        )
+
+    def e_relay(k):
+        owner = e_owner(k)
+        e_core(k).wait_recv()
+
+        def one(z_at):
+            e_p[owner, z_at] = (e_send[core, owner, z_at].astype(F32) + e_rc[owner, z_at].astype(F32)).astype(BF16)
+
+        loop(0, nz, one)
+        loop(1, nz, lambda j: e_sum(k, j).start())
+
     load_we.wait()
     load_cot.wait()
     expand_block(0)
     weight_relay(1)
     expand_back(0)
+    e_core(0).start()
     weight_relay(3)
     weight_core(1).wait_recv()
     expand_block(1)
     weight_relay(2)
+    e_relay(0)
     weight_core(3).wait_recv()
     expand_block(3)
     cot_y(1).wait_recv()
     expand_back(1)
+    e_core(1).start()
     weight_core(2).wait_recv()
     expand_block(2)
+    e_relay(1)
     cot_y(3).wait_recv()
     expand_back(3)
+    e_core(3).start()
     cot_y(2).wait_recv()
     out_y(1).start()
     out_y(3).start()
     expand_back(2)
+    e_core(2).start()
 
     def core_sum(send, got, k):
         return remote(send.at[1 - core], got, c_send_sem.at[k], c_recv_sem.at[k], other_core)
@@ -296,9 +325,6 @@
 
         return lax.fori_loop(1, nz, one, src[z].astype(F32))
 
-    e_core = core_sum(e_send, e_rc, 4)
-    e_core.start()
-
     spre = spre_s[...]
     sig = sigmoid(spre)
     sgrad_pre = stg[:, 0:mid] * slope_of(spre, sig)
@@ -311,21 +337,60 @@
 
     s_rows = mid * 3 // planes
     flat = sgp[0:half_rows].reshape(pix, mid)
+
+    def s_core(r):
+        at = slice(r * s_rows, (r + 1) * s_rows)
+        return remote(
+            s_send.at[1 - core, :, :, at], s_rc.at[:, :, at], e_send_sem.at[r * nz], e_recv_sem.at[r * nz], other_core
+        )
+
     for r in range(3):
         term = dot_tn(windows(r), flat).astype(BF16)
         for h in range(2):
             for q in range(planes):
-                s_send[h, q, r * s_rows : (r + 1) * s_rows] = term[
+                s_send[h, q // 4, q % 4, r * s_rows : (r + 1) * s_rows] = term[
                     q * s_rows : (q + 1) * s_rows, h * lanes : (h + 1) * lanes
                 ]
-    s_core = core_sum(s_send, s_rc, 5)
-    s_core.start()
-    e_core.wait_recv()
-    add_core(e_send, e_rc, e_p)
-    loop(1, nz, lambda k: z_sum(e_p, e_rp, 0, k).start())
-    s_core.wait_recv()
-    add_core(s_send, s_rc, s_p)
-    loop(1, planes, lambda k: plane_sum(s_p, s_rp, 1, k).start())
+        s_core(r).start()
+    e_relay(3)
+
+    def add_spatial(at):
+        def one(q):
+            x_at, y_at = q // 4, q % 4
+            s_p[x_at, y_at, at] = (s_send[core, x_at, y_at, at].astype(F32) + s_rc[x_at, y_at, at].astype(F32)).astype(BF16)
+
+        loop(0, planes, one)
+
+    a_rows, b_rows = 2 * s_rows, s_rows
+
+    def over_x(src, dst, group, k):
+        slot = 4 * group + k
+        return remote(src, dst, q_send_sem.at[slot], q_recv_sem.at[slot], at_x((x + k) % nx))
+
+    def over_y(src, dst, group, k):
+        slot = 4 * group + k
+        return remote(src, dst, q_send_sem.at[slot], q_recv_sem.at[slot], at_y((y + k) % 4))
+
+    def s_a_first(k):
+        return over_x(s_p.at[(x + k) % nx, :, 0:a_rows], s_a1.at[k], 0, k)
+
+    def s_b_first(k):
+        return over_y(s_p.at[:, (y + k) % 4, a_rows : a_rows + b_rows], s_b1.at[k], 1, k)
+
+    def s_a_second(k):
+        return over_y(s_am.at[(y + k) % 4], s_a2.at[k], 2, k)
+
+    def s_b_second(k):
+        return over_x(s_bm.at[(x + k) % nx], s_b2.at[k], 3, k)
+
+    s_core(0).wait_recv()
+    s_core(1).wait_recv()
+    add_spatial(slice(0, a_rows))
+    loop(1, nx, lambda k: s_a_first(k).start())
+    s_core(2).wait_recv()
+    add_spatial(slice(a_rows, a_rows + b_rows))
+    loop(1, 4, lambda k: s_b_first(k).start())
+    e_relay(2)
 
     @pl.when(y < 3)
     def _():
@@ -379,13 +444,8 @@
     for h in range(2):
         for q in range(planes):
             r_send[h, q] = rterm[q * r_rows : (q + 1) * r_rows, h * lanes : (h + 1) * lanes].astype(BF16)
-    r_core = core_sum(r_send, r_rc, 6)
+    r_core = core_sum(r_send, r_rc, 9)
     r_core.start()
-
-    out_y(2).start()
-    r_core.wait_recv()
-    add_core(r_send, r_rc, r_p)
-    loop(1, planes, lambda k: plane_sum(r_p, r_rp, 2, k).start())
 
     def input_row(p):
         wide = dot_nt(rgp_s[p], wr[...])
@@ -406,16 +466,52 @@
                 )
                 igrad[p, :, lane] = widebuf[block].astype(BF16)
 
-    loop(0, rows, input_row)
+    loop(0, half_rows, input_row)
+    r_core.wait_recv()
+    add_core(r_send, r_rc, r_p)
+    loop(1, planes, lambda k: plane_sum(r_p, r_rp, 2, k).start())
+
+    loop(1, nx, lambda k: s_a_first(k).wait_recv())
+    for y_at in range(4):
+        total = s_p[x, y_at, 0:a_rows].astype(F32)
+        for k in range(1, nx):
+            total = total + s_a1[k, y_at].astype(F32)
+        s_am[y_at] = total.astype(BF16)
+    loop(1, 4, lambda k: s_a_second(k).start())
+    loop(1, 4, lambda k: s_b_first(k).wait_recv())
+    for x_at in range(nx):
+        total = s_p[x_at, y, a_rows : a_rows + b_rows].astype(F32)
+        for k in range(1, 4):
+            total = total + s_b1[k, x_at].astype(F32)
+        s_bm[x_at] = total.astype(BF16)
+    loop(1, nx, lambda k: s_b_second(k).start())
+    loop(half_rows, rows, input_row)
 
     st_rows, rt_rows, t_rows = 3 * s_rows, r_rows, t_z.shape[0] * t_z.shape[1]
-    total = [plane_total(s_p, s_rp, 1), plane_total(r_p, r_rp, 2)]
+    total_a = s_am[y].astype(F32)
+    for k in range(1, 4):
+        s_a_second(k).wait_recv()
+        total_a = total_a + s_a2[k].astype(F32)
+    total_b = s_bm[x].astype(F32)
+    for k in range(1, nx):
+        s_b_second(k).wait_recv()
+        total_b = total_b + s_b2[k].astype(F32)
+    total = [total_a, total_b, plane_total(r_p, r_rp, 2)]
     if t_rows > st_rows + rt_rows:
         total.append(jnp.zeros((t_rows - st_rows - rt_rows, lanes), F32))
     t_z[...] = jnp.concatenate(total, axis=0).reshape(t_z.shape)
     loop(1, nz, lambda k: z_sum(t_z, t_rz, 2, k).start())
 
-    e_z[...] = z_total(e_p, e_rp, 0).reshape(e_z.shape)
+    out_y(2).start()
+
+    for k in range(4):
+        owner = e_owner(k)
+
+        def e_add(j, total):
+            e_sum(k, j).wait_recv()
+            return total + e_rp[owner, j].astype(F32)
+
+        e_z[owner] = lax.fori_loop(1, nz, e_add, e_p[owner, z].astype(F32)).reshape(e_z.shape[1:])
 
     def e_plane(k):
         place = (plane + k) % planes
@@ -441,25 +537,68 @@
 
     loop(1, nx, lambda k: e_x(k).start())
 
+    @pl.when(y < 3)
+    def _():
+        halo_row.wait_send()
+
+    @pl.when(y > 0)
+    def _():
+        halo_grad.wait_send()
+
+    for k in range(1, 4):
+        weight_y(k).wait_send()
+        cot_y(k).wait_send()
+        loop(1, nx, lambda j: weight_x(k, j).wait_send())
+        weight_core(k).wait_send()
+    for k in range(4):
+        e_core(k).wait_send()
+        loop(1, nz, lambda j: e_sum(k, j).wait_send())
+    for r in range(3):
+        s_core(r).wait_send()
+    r_core.wait_send()
+    loop(1, planes, lambda k: plane_sum(r_p, r_rp, 2, k).wait_send())
+    for k in range(1, 4):
+        if k < nx:
+            s_a_first(k).wait_send()
+            s_b_second(k).wait_send()
+        s_b_first(k).wait_send()
+        s_a_second(k).wait_send()
+
     loop(1, nz, lambda k: z_spread(t_f, t_g, 4, k).wait_recv())
     t_g[z] = t_f[...]
-    t_out[core, plane] = t_g[...].reshape(t_rows, lanes).astype(BF16)
-
-    def t_spread(k):
-        slot = 4 * planes + k
-        return remote(
-            t_out.at[core, plane], t_out.at[core, plane], p_send_sem.at[slot], p_recv_sem.at[slot], at_plane((plane + k) % planes)
-        )
-
-    def t_cross(k):
-        place = (plane + planes - k) % planes
-        return remote(
-            t_out.at[core, place], t_out.at[core, place], c_send_sem.at[8 + k], c_recv_sem.at[8 + k], other_core
-        )
-
-    loop(1, planes, lambda k: t_spread(k).start())
-    t_cross(0).start()
-
+    t_out[core, x, y] = t_g[...].reshape(t_rows, lanes).astype(BF16)
+
+    part_a, part_b = slice(0, a_rows), slice(a_rows, t_rows)
+
+    def t_a_first(k):
+        return over_y(t_out.at[core, x, y, part_a], t_out.at[core, x, y, part_a], 4, k)
+
+    def t_b_first(k):
+        return over_x(t_out.at[core, x, y, part_b], t_out.at[core, x, y, part_b], 5, k)
+
+    def t_a_second(k):
+        return over_x(t_out.at[core, x, :, part_a], t_out.at[core, x, :, part_a], 6, k)
+
+    def t_b_second(k):
+        return over_y(t_out.at[core, :, y, part_b], t_out.at[core, :, y, part_b], 7, k)
+
+    def t_a_cross(k):
+        at = t_out.at[core, (x + nx - k) % nx, :, part_a]
+        return remote(at, at, c_send_sem.at[11 + k], c_recv_sem.at[11 + k], other_core)
+
+    def t_b_cross(k):
+        at = t_out.at[core, :, (y + 4 - k) % 4, part_b]
+        return remote(at, at, c_send_sem.at[15 + k], c_recv_sem.at[15 + k], other_core)
+
+    loop(1, 4, lambda k: t_a_first(k).start())
+    loop(1, nx, lambda k: t_b_first(k).start())
+
+    loop(1, 4, lambda k: t_a_first(k).wait_recv())
+    loop(1, nx, lambda k: t_a_second(k).start())
+    loop(1, nx, lambda k: t_b_first(k).wait_recv())
+    loop(1, 4, lambda k: t_b_second(k).start())
+    t_a_cross(0).start()
+    t_b_cross(0).start()
     loop(1, nx, lambda k: e_x(k).wait_recv())
     e_g[x] = e_f[...]
     e_out[core, z] = e_g[...].reshape(e_rows, lanes).astype(BF16)
@@ -472,22 +611,23 @@
 
     loop(1, nz, lambda k: e_back(k).start())
 
-    def pass_on(k):
-        t_spread(k).wait_recv()
-        t_cross(k).start()
-
-    loop(1, planes, pass_on)
+    for k in (1, 3, 2):
+        if k < nx:
+            t_a_second(k).wait_recv()
+            t_a_cross(k).start()
+        t_b_second(k).wait_recv()
+        t_b_cross(k).start()
     loop(1, nz, lambda k: e_back(k).wait())
-    e_cross = remote(e_out.at[core], e_out.at[core], c_send_sem.at[7], c_recv_sem.at[7], other_core)
+    e_cross = remote(e_out.at[core], e_out.at[core], c_send_sem.at[10], c_recv_sem.at[10], other_core)
     e_cross.start()
 
     def finish_place(h, q):
         lane = slice(h * lanes, (h + 1) * lanes)
         for r in range(3):
             rows_at = pl.ds(pl.multiple_of(q * s_rows, s_rows), s_rows)
-            sgrad[r, rows_at, lane] = t_out[h, q, r * s_rows : (r + 1) * s_rows].astype(F32) * scale
+            sgrad[r, rows_at, lane] = t_out[h, q // 4, q % 4, r * s_rows : (r + 1) * s_rows].astype(F32) * scale
         rows_at = pl.ds(pl.multiple_of(q * r_rows, r_rows), r_rows)
-        rgrad[rows_at, lane] = t_out[h, q, st_rows : st_rows + r_rows].astype(F32) * scale
+        rgrad[rows_at, lane] = t_out[h, q // 4, q % 4, st_rows : st_rows + r_rows].astype(F32) * scale
 
     for h in range(2):
 
@@ -495,7 +635,8 @@
         def _():
             loop(0, planes, lambda q: finish_place(h, q))
 
-    loop(0, planes, lambda k: t_cross(k).wait_recv())
+    loop(0, nx, lambda k: t_a_cross(k).wait_recv())
+    loop(0, 4, lambda k: t_b_cross(k).wait_recv())
     for h in range(2):
 
         @pl.when(core != h)
@@ -507,42 +648,41 @@
         for z_at in range(nz):
             egrad[z_at * e_rows : (z_at + 1) * e_rows, h * lanes : (h + 1) * lanes] = e_out[h, z_at].astype(F32) * scale
 
-    @pl.when(y < 3)
-    def _():
-        halo_row.wait_send()
-
-    @pl.when(y > 0)
-    def _():
-        halo_grad.wait_send()
-
-    def finish_y(k):
-        weight_y(k).wait_send()
-        cot_y(k).wait_send()
+    for k in range(1, 4):
         out_y(k).wait()
-
-    loop(1, 4, finish_y)
-    for k in range(1, 4):
-        loop(1, nx, lambda j: weight_x(k, j).wait_send())
-        weight_core(k).wait_send()
-    for copy in (e_core, s_core, r_core, e_cross):
-        copy.wait_send()
-    loop(1, nx, lambda k: e_x(k).wait_send())
-
-    def finish_plane(k):
-        e_plane(k).wait_send()
-        plane_sum(s_p, s_rp, 1, k).wait_send()
-        plane_sum(r_p, r_rp, 2, k).wait_send()
-        t_spread(k).wait_send()
-
-    loop(1, planes, finish_plane)
+        t_a_first(k).wait_send()
+        t_b_second(k).wait_send()
+        t_b_cross(k).wait_send()
+        if k < nx:
+            e_x(k).wait_send()
+            t_b_first(k).wait_send()
+            t_a_second(k).wait_send()
+            t_a_cross(k).wait_send()
+    t_a_cross(0).wait_send()
+    t_b_cross(0).wait_send()
+    e_cross.wait_send()
+    loop(1, planes, lambda k: e_plane(k).wait_send())
 
     def finish_z(k):
-        z_sum(e_p, e_rp, 0, k).wait_send()
         z_sum(t_z, t_rz, 2, k).wait_send()
         z_spread(t_f, t_g, 4, k).wait_send()
 
     loop(1, nz, finish_z)
-    loop(0, planes, lambda k: t_cross(k).wait_send())
+
+
+def place_kernel(cuts, *refs):
+    count = len(cuts)
+    sources, targets, sem = refs[:count], refs[count : 2 * count], refs[2 * count]
+    copies = []
+    for source, target, pieces in zip(sources, targets, cuts):
+        size = source.shape[0] // pieces
+        for piece in range(pieces):
+            at = pl.ds(piece * size, size)
+            copies.append(pltpu.make_async_copy(source.at[at], target.at[at], sem.at[len(copies)]))
+    for copy in copies:
+        copy.start()
+    for copy in copies:
+        copy.wait()
 
 
 def body(nx, nz, images, reduce_weight, spatial_weight, expand_weight, cotangent):
@@ -557,6 +697,7 @@
     e_rows = stack_ch // nz
     f_rows = e_rows // nx
     s_rows = 9 * mid // planes
+    a_rows, b_rows = s_rows // 3 * 2, s_rows // 3
     r_rows = chans // planes
     t_rows = -(-(s_rows + r_rows) // (8 * nz)) * 8 * nz
     cot_blocks = cotangent[0].reshape(4, pix, filt)
@@ -585,19 +726,24 @@
         V((rows, cols, mid), BF16),
         V((chans, mid), F32),
         V((chans // lanes, cols, lanes), F32),
-        V((2, nz, 4, e_rows, lanes), BF16),
-        V((nz, 4, e_rows, lanes), BF16),
-        V((nz, 4, e_rows, lanes), BF16),
-        V((nz, 4, e_rows, lanes), BF16),
+        V((2, 4, nz, e_rows, lanes), BF16),
+        V((4, nz, e_rows, lanes), BF16),
+        V((4, nz, e_rows, lanes), BF16),
+        V((4, nz, e_rows, lanes), BF16),
         V((4, nx, f_rows, lanes), F32),
         V((planes, f_rows, lanes), F32),
         V((f_rows, lanes), F32),
         V((nx, f_rows, lanes), F32),
         V((2, nz, e_rows, lanes), BF16),
-        V((2, planes, s_rows, lanes), BF16),
-        V((planes, s_rows, lanes), BF16),
-        V((planes, s_rows, lanes), BF16),
-        V((planes, s_rows, lanes), BF16),
+        V((2, nx, 4, s_rows, lanes), BF16),
+        V((nx, 4, s_rows, lanes), BF16),
+        V((nx, 4, s_rows, lanes), BF16),
+        V((nx, 4, a_rows, lanes), BF16),
+        V((4, a_rows, lanes), BF16),
+        V((4, a_rows, lanes), BF16),
+        V((4, nx, b_rows, lanes), BF16),
+        V((nx, b_rows, lanes), BF16),
+        V((nx, b_rows, lanes), BF16),
         V((2, planes, r_rows, lanes), BF16),
         V((planes, r_rows, lanes), BF16),
         V((planes, r_rows, lanes), BF16),
@@ -606,20 +752,24 @@
         V((nz, t_rows // nz, lanes), F32),
         V((t_rows // nz, lanes), F32),
         V((nz, t_rows // nz, lanes), F32),
-        V((2, planes, t_rows, lanes), BF16),
+        V((2, nx, 4, t_rows, lanes), BF16),
         D((14,)),
         D((14,)),
         D((5 * planes,)),
         D((5 * planes,)),
         D((5 * nz,)),
         D((5 * nz,)),
-        D((8 + planes,)),
-        D((8 + planes,)),
+        D((19,)),
+        D((19,)),
         D((4 * nx,)),
         D((4 * nx,)),
+        D((4 * nz,)),
+        D((4 * nz,)),
+        D((32,)),
+        D((32,)),
         D((rows + 4,)),
     ]
-    output, input_grad, reduce_grad, spatial_grad, expand_grad = pl.pallas_call(
+    results = pl.pallas_call(
         functools.partial(block_kernel, nx, nz),
         out_shape=(
             pltpu.VMEM((4, pix, filt), BF16),
@@ -635,6 +785,15 @@
             collective_id=0, has_side_effects=True, vmem_limit_bytes=48 * 1024 * 1024
         ),
     )(image, reduce_weight, weights, expand_weight, cot_blocks)
+    cuts = (2, 4, 1, 3, 2)
+    output, input_grad, reduce_grad, spatial_grad, expand_grad = pl.pallas_call(
+        functools.partial(place_kernel, cuts),
+        out_shape=[jax.ShapeDtypeStruct(result.shape, result.dtype) for result in results],
+        in_specs=[pl.BlockSpec(memory_space=pl.ANY)] * 5,
+        out_specs=[pl.BlockSpec(memory_space=pl.ANY)] * 5,
+        scratch_shapes=[D((sum(cuts),))],
+        compiler_params=pltpu.CompilerParams(vmem_limit_bytes=2 * 1024 * 1024),
+    )(*results)
     return (
         output.reshape((1, 4 * half_rows, half_cols, filt)),
         input_grad[None],

time: 90.4 us -> 84.6 us (0.936)
  local copies, waits for them, and re-layouts: 5.37 us -> 0 us
    unnamed x5 -> x0, local copies, waits for them, and re-layouts: 5.37 us -> none
    pallas_call x1, Pallas kernels: 84.3 us -> 80.9 us  [body(): pl.pallas_call(functools.partial(block_kernel, nx, nz), out_shape=(pltpu....]
    pallas_call x0 -> x1, Pallas kernels: none -> 2.91 us  [body(): pl.pallas_call(functools.partial(place_kernel, cuts), out_shape=[jax.Shap...]
where the time goes in v3:
time: 84.6 us; the launch traced here: 84.5 us
  Pallas kernels  83.9 us (99%)
    pallas_call x1, Pallas kernels, body(): pl.pallas_call(functools.partial(block_kernel, nx, nz), out_shape=(pltpu....  80.9 us
    pallas_call x1, Pallas kernels, body(): pl.pallas_call(functools.partial(place_kernel, cuts), out_shape=[jax.Shap...  2.91 us

profile of v3, /device:TPU:1, one launch (start us, length us, event | category | flops | bytes accessed | tf_op | source)
XLA Modules:
  0.0 84.5 jit_solution(326262277238410499)
XLA Ops:
  0.6 80.9 %shard_map.92 = (bf16[4,512,256]{2,1,0:T(8,128)(2,1)S(1)}, bf16[8,256,512]{2,1,0:T(8,128)(2,1)S(1)}, f32[512,256]{1,0:T(8,128)S(1)}, f32[3,768,256]{2,1,0:T(8,128)S(1)}, f32[768,256]{1,0:T(8,128)S(1)}) custom-call(bf16[8,256,512]{2,1,0:T(8,128)(2,1)} %bitcast.6, bf16[512,256]{1,0:T(8,128)(2,1)} %wr_hbm.1, bf16[3,768,256]{2,1,0:T(8,128)(2,1)} %bitcast.7, ...), custom_call_target="tpu_custom_call" | custom-call | tf_op jit(solution)/shard_map/pallas_call | solution.py:772
  81.6 2.9 %shard_map.93 = (bf16[4,512,256]{2,1,0:T(8,128)(2,1)}, bf16[8,256,512]{2,1,0:T(8,128)(2,1)}, f32[512,256]{1,0:T(8,128)}, f32[3,768,256]{2,1,0:T(8,128)}, f32[768,256]{1,0:T(8,128)}) custom-call(bf16[4,512,256]{2,1,0:T(8,128)(2,1)S(1)} %get-tuple-element.15.refs_0_, bf16[8,256,512]{2,1,0:T(8,128)(2,1)S(1)} %get-tuple-element.16.refs_1_, ...), custom_call_target="tpu_custom_call" | custom-call | tf_op jit(solution)/shard_map/pallas_call | solution.py:789

commit v4 on v3

--- a/solution.py
+++ b/solution.py
@@ -284,6 +284,7 @@
     out_y(3).start()
     expand_back(2)
     e_core(2).start()
+    e_relay(3)
 
     def core_sum(send, got, k):
         return remote(send.at[1 - core], got, c_send_sem.at[k], c_recv_sem.at[k], other_core)
@@ -337,13 +338,6 @@
 
     s_rows = mid * 3 // planes
     flat = sgp[0:half_rows].reshape(pix, mid)
-
-    def s_core(r):
-        at = slice(r * s_rows, (r + 1) * s_rows)
-        return remote(
-            s_send.at[1 - core, :, :, at], s_rc.at[:, :, at], e_send_sem.at[r * nz], e_recv_sem.at[r * nz], other_core
-        )
-
     for r in range(3):
         term = dot_tn(windows(r), flat).astype(BF16)
         for h in range(2):
@@ -351,15 +345,16 @@
                 s_send[h, q // 4, q % 4, r * s_rows : (r + 1) * s_rows] = term[
                     q * s_rows : (q + 1) * s_rows, h * lanes : (h + 1) * lanes
                 ]
-        s_core(r).start()
-    e_relay(3)
-
-    def add_spatial(at):
-        def one(q):
-            x_at, y_at = q // 4, q % 4
-            s_p[x_at, y_at, at] = (s_send[core, x_at, y_at, at].astype(F32) + s_rc[x_at, y_at, at].astype(F32)).astype(BF16)
-
-        loop(0, planes, one)
+    s_core = core_sum(s_send, s_rc, 8)
+    s_core.start()
+    e_relay(2)
+    s_core.wait_recv()
+
+    def add_spatial(q):
+        x_at, y_at = q // 4, q % 4
+        s_p[x_at, y_at] = (s_send[core, x_at, y_at].astype(F32) + s_rc[x_at, y_at].astype(F32)).astype(BF16)
+
+    loop(0, planes, add_spatial)
 
     a_rows, b_rows = 2 * s_rows, s_rows
 
@@ -383,14 +378,8 @@
     def s_b_second(k):
         return over_x(s_bm.at[(x + k) % nx], s_b2.at[k], 3, k)
 
-    s_core(0).wait_recv()
-    s_core(1).wait_recv()
-    add_spatial(slice(0, a_rows))
     loop(1, nx, lambda k: s_a_first(k).start())
-    s_core(2).wait_recv()
-    add_spatial(slice(a_rows, a_rows + b_rows))
     loop(1, 4, lambda k: s_b_first(k).start())
-    e_relay(2)
 
     @pl.when(y < 3)
     def _():
@@ -444,33 +433,6 @@
     for h in range(2):
         for q in range(planes):
             r_send[h, q] = rterm[q * r_rows : (q + 1) * r_rows, h * lanes : (h + 1) * lanes].astype(BF16)
-    r_core = core_sum(r_send, r_rc, 9)
-    r_core.start()
-
-    def input_row(p):
-        wide = dot_nt(rgp_s[p], wr[...])
-
-        @pl.when(p % 2 == 1)
-        def _():
-            igrad[p] = wide.astype(BF16)
-
-        @pl.when(p % 2 == 0)
-        def _():
-            first = pl.ds(pl.multiple_of((p // 2) * half_cols, half_cols), half_cols)
-            for block in range(chans // lanes):
-                lane = slice(block * lanes, (block + 1) * lanes)
-                widebuf[block] = wide[:, lane]
-                widebuf[block, pl.ds(0, half_cols, stride=2), :] = (
-                    widebuf[block, pl.ds(0, half_cols, stride=2), :]
-                    + stg[first, mid + block * lanes : mid + (block + 1) * lanes]
-                )
-                igrad[p, :, lane] = widebuf[block].astype(BF16)
-
-    loop(0, half_rows, input_row)
-    r_core.wait_recv()
-    add_core(r_send, r_rc, r_p)
-    loop(1, planes, lambda k: plane_sum(r_p, r_rp, 2, k).start())
-
     loop(1, nx, lambda k: s_a_first(k).wait_recv())
     for y_at in range(4):
         total = s_p[x, y_at, 0:a_rows].astype(F32)
@@ -485,7 +447,33 @@
             total = total + s_b1[k, x_at].astype(F32)
         s_bm[x_at] = total.astype(BF16)
     loop(1, nx, lambda k: s_b_second(k).start())
-    loop(half_rows, rows, input_row)
+    r_core = core_sum(r_send, r_rc, 9)
+    r_core.start()
+
+    r_core.wait_recv()
+    add_core(r_send, r_rc, r_p)
+    loop(1, planes, lambda k: plane_sum(r_p, r_rp, 2, k).start())
+
+    def input_row(p):
+        wide = dot_nt(rgp_s[p], wr[...])
+
+        @pl.when(p % 2 == 1)
+        def _():
+            igrad[p] = wide.astype(BF16)
+
+        @pl.when(p % 2 == 0)
+        def _():
+            first = pl.ds(pl.multiple_of((p // 2) * half_cols, half_cols), half_cols)
+            for block in range(chans // lanes):
+                lane = slice(block * lanes, (block + 1) * lanes)
+                widebuf[block] = wide[:, lane]
+                widebuf[block, pl.ds(0, half_cols, stride=2), :] = (
+                    widebuf[block, pl.ds(0, half_cols, stride=2), :]
+                    + stg[first, mid + block * lanes : mid + (block + 1) * lanes]
+                )
+                igrad[p, :, lane] = widebuf[block].astype(BF16)
+
+    loop(0, rows, input_row)
 
     st_rows, rt_rows, t_rows = 3 * s_rows, r_rows, t_z.shape[0] * t_z.shape[1]
     total_a = s_am[y].astype(F32)
@@ -537,33 +525,6 @@
 
     loop(1, nx, lambda k: e_x(k).start())
 
-    @pl.when(y < 3)
-    def _():
-        halo_row.wait_send()
-
-    @pl.when(y > 0)
-    def _():
-        halo_grad.wait_send()
-
-    for k in range(1, 4):
-        weight_y(k).wait_send()
-        cot_y(k).wait_send()
-        loop(1, nx, lambda j: weight_x(k, j).wait_send())
-        weight_core(k).wait_send()
-    for k in range(4):
-        e_core(k).wait_send()
-        loop(1, nz, lambda j: e_sum(k, j).wait_send())
-    for r in range(3):
-        s_core(r).wait_send()
-    r_core.wait_send()
-    loop(1, planes, lambda k: plane_sum(r_p, r_rp, 2, k).wait_send())
-    for k in range(1, 4):
-        if k < nx:
-            s_a_first(k).wait_send()
-            s_b_second(k).wait_send()
-        s_b_first(k).wait_send()
-        s_a_second(k).wait_send()
-
     loop(1, nz, lambda k: z_spread(t_f, t_g, 4, k).wait_recv())
     t_g[z] = t_f[...]
     t_out[core, x, y] = t_g[...].reshape(t_rows, lanes).astype(BF16)
@@ -648,26 +609,54 @@
         for z_at in range(nz):
             egrad[z_at * e_rows : (z_at + 1) * e_rows, h * lanes : (h + 1) * lanes] = e_out[h, z_at].astype(F32) * scale
 
+    @pl.when(y < 3)
+    def _():
+        halo_row.wait_send()
+
+    @pl.when(y > 0)
+    def _():
+        halo_grad.wait_send()
+
+    def finish_y(k):
+        weight_y(k).wait_send()
+        cot_y(k).wait_send()
+        out_y(k).wait()
+
+    loop(1, 4, finish_y)
     for k in range(1, 4):
-        out_y(k).wait()
-        t_a_first(k).wait_send()
-        t_b_second(k).wait_send()
-        t_b_cross(k).wait_send()
-        if k < nx:
-            e_x(k).wait_send()
-            t_b_first(k).wait_send()
-            t_a_second(k).wait_send()
-            t_a_cross(k).wait_send()
-    t_a_cross(0).wait_send()
-    t_b_cross(0).wait_send()
-    e_cross.wait_send()
-    loop(1, planes, lambda k: e_plane(k).wait_send())
+        loop(1, nx, lambda j: weight_x(k, j).wait_send())
+        weight_core(k).wait_send()
+    for copy in (s_core, r_core, e_cross):
+        copy.wait_send()
+    loop(1, nx, lambda k: e_x(k).wait_send())
+
+    def finish_plane(k):
+        e_plane(k).wait_send()
+        plane_sum(r_p, r_rp, 2, k).wait_send()
+
+    loop(1, planes, finish_plane)
 
     def finish_z(k):
         z_sum(t_z, t_rz, 2, k).wait_send()
         z_spread(t_f, t_g, 4, k).wait_send()
 
     loop(1, nz, finish_z)
+
+    def finish_x(k):
+        for copy in (s_a_first(k), s_b_second(k), t_b_first(k), t_a_second(k)):
+            copy.wait_send()
+
+    def finish_q(k):
+        for copy in (s_b_first(k), s_a_second(k), t_a_first(k), t_b_second(k)):
+            copy.wait_send()
+
+    loop(1, nx, finish_x)
+    loop(1, 4, finish_q)
+    loop(0, nx, lambda k: t_a_cross(k).wait_send())
+    loop(0, 4, lambda k: t_b_cross(k).wait_send())
+    for k in range(4):
+        e_core(k).wait_send()
+        loop(1, nz, lambda j: e_sum(k, j).wait_send())
 
 
 def place_kernel(cuts, *refs):

time: 84.6 us -> 83.9 us (level)
  no operation moved by 1% of the time
where the time goes in v4:
time: 83.9 us; the launch traced here: 83.8 us
  Pallas kernels  83.2 us (99%)
    pallas_call x1, Pallas kernels, body(): pl.pallas_call(functools.partial(block_kernel, nx, nz), out_shape=(pltpu....  80.3 us
    pallas_call x1, Pallas kernels, body(): pl.pallas_call(functools.partial(place_kernel, cuts), out_shape=[jax.Shap...  2.91 us

profile of v4, /device:TPU:1, one launch (start us, length us, event | category | flops | bytes accessed | tf_op | source)
XLA Modules:
  0.0 83.8 jit_solution(4216254993249102108)
XLA Ops:
  0.6 80.3 %shard_map.92 = (bf16[4,512,256]{2,1,0:T(8,128)(2,1)S(1)}, bf16[8,256,512]{2,1,0:T(8,128)(2,1)S(1)}, f32[512,256]{1,0:T(8,128)S(1)}, f32[3,768,256]{2,1,0:T(8,128)S(1)}, f32[768,256]{1,0:T(8,128)S(1)}) custom-call(bf16[8,256,512]{2,1,0:T(8,128)(2,1)} %bitcast.6, bf16[512,256]{1,0:T(8,128)(2,1)} %wr_hbm.1, bf16[3,768,256]{2,1,0:T(8,128)(2,1)} %bitcast.7, ...), custom_call_target="tpu_custom_call" | custom-call | tf_op jit(solution)/shard_map/pallas_call | solution.py:761
  80.9 2.9 %shard_map.93 = (bf16[4,512,256]{2,1,0:T(8,128)(2,1)}, bf16[8,256,512]{2,1,0:T(8,128)(2,1)}, f32[512,256]{1,0:T(8,128)}, f32[3,768,256]{2,1,0:T(8,128)}, f32[768,256]{1,0:T(8,128)}) custom-call(bf16[4,512,256]{2,1,0:T(8,128)(2,1)S(1)} %get-tuple-element.15.refs_0_, bf16[8,256,512]{2,1,0:T(8,128)(2,1)S(1)} %get-tuple-element.16.refs_1_, ...), custom_call_target="tpu_custom_call" | custom-call | tf_op jit(solution)/shard_map/pallas_call | solution.py:778
